TPU v7x, 256 devices: a whole 4x4x8 slice. The times are simulated.
256 devices in a mesh: seq: 16 (over y, x_lo, core), tp: 16 (over x_hi, z).
Axes of the slice: x: 4 (x_hi: 2, x_lo: 2; x = x_hi * 2 + x_lo), y: 4, z: 8, core: 2. Of those that a mesh axis runs over, the one named last changes fastest.
Arguments:
- tokens: bfloat16 [6144, 4096], P('seq'), may hold values from -14 to 14
- w_query: bfloat16 [4096, 4096], P(None, 'tp'), may hold values from -0.09375 to 0.09375
- w_key: bfloat16 [4096, 4096], P(None, 'tp'), may hold values from -0.09375 to 0.09375
- w_value: bfloat16 [4096, 4096], P(None, 'tp'), may hold values from -0.09375 to 0.09375
- grad_out: bfloat16 [6144, 4096], P('seq', 'tp'), may hold values from -6 to 6
Outputs:
- grad_tokens: bfloat16 [6144, 4096], P('seq')
All inputs are finite; a program needn't handle non-finite values.
Results may differ from a plain program's by a relative error of at most 0.03.
Values may be sent and summed in bfloat16 or wider, within the bound.
A program may use at most 128 MiB of HBM per device.

v0:
```python
import jax
import jax.numpy as jnp
from jax import lax
from jax.sharding import PartitionSpec as P

HEAD = 128


def shifted(block, axis, distance):
    devices = range(lax.axis_size(axis))
    route = [((i - distance) % len(devices), i) for i in devices]
    return lax.ppermute(block, axis, route)


def shards(tokens, w_query, w_key, w_value, grad_out):
    rows = tokens.shape[0]
    local_heads = w_query.shape[1] // HEAD
    score_scale = HEAD ** (-0.5)
    cycle_size = lax.axis_size("seq")
    own_index = lax.axis_index("seq")

    def project(weight):
        product = jnp.dot(tokens, weight, preferred_element_type=jnp.float32).astype(jnp.bfloat16)
        return product.reshape(rows, local_heads, HEAD)

    queries = project(w_query)
    paired = jnp.stack((project(w_key), project(w_value)))
    grad_heads = grad_out.reshape(rows, local_heads, HEAD)
    offsets = jnp.arange(rows, dtype=jnp.int32) * cycle_size
    query_times = offsets + own_index

    def block_scores(key_block, source):
        scores = (
            jnp.einsum("qhd,khd->hqk", queries, key_block, preferred_element_type=jnp.float32)
            * score_scale
        )
        allowed = (offsets + source)[None, :] <= query_times[:, None]
        return jnp.where(allowed[None], scores, -1e30)

    def forward_step(running, pair, source):
        top, total, summed = running
        scores = block_scores(pair[0], source)
        new_top = jnp.maximum(top, jnp.max(scores, axis=2))
        factor = jnp.exp(top - new_top)
        weights = jnp.exp(scores - new_top[..., None])
        total = total * factor + jnp.sum(weights, axis=2)
        update = jnp.einsum(
            "hqk,khd->hqd",
            weights.astype(jnp.bfloat16),
            pair[1],
            preferred_element_type=jnp.float32,
        )
        summed = summed * factor[..., None] + update
        return (new_top, total, summed)

    start_state = (
        jnp.full((local_heads, rows), -1e30, jnp.float32),
        jnp.zeros((local_heads, rows), jnp.float32),
        jnp.zeros((local_heads, rows, HEAD), jnp.float32),
    )

    def cycle_forward(step, carry):
        pair, running = carry
        pair = shifted(pair, "seq", 1)
        source = (own_index - step) % cycle_size
        return (pair, forward_step(running, pair, source))

    first = forward_step(start_state, paired, own_index)
    unused, running = lax.fori_loop(1, cycle_size, cycle_forward, (paired, first))
    top, total, summed = running
    logsum = top + jnp.log(total)
    attended = (summed / total[..., None]).astype(jnp.bfloat16)
    row_delta = jnp.sum(
        grad_heads.astype(jnp.float32) * jnp.transpose(attended, (1, 0, 2)).astype(jnp.float32),
        axis=2,
    ).T

    def backward_step(pair, source):
        key_block = pair[0]
        value_block = pair[1]
        scores = block_scores(key_block, source)
        probs = jnp.exp(scores - logsum[..., None])
        grad_value = jnp.einsum(
            "hqk,qhd->khd",
            probs.astype(jnp.bfloat16),
            grad_heads,
            preferred_element_type=jnp.float32,
        )
        grad_probs = jnp.einsum(
            "qhd,khd->hqk", grad_heads, value_block, preferred_element_type=jnp.float32
        )
        grad_scores = (probs * (grad_probs - row_delta[..., None])).astype(jnp.bfloat16)
        grad_query = jnp.einsum(
            "hqk,khd->qhd", grad_scores, key_block, preferred_element_type=jnp.float32
        )
        grad_key = jnp.einsum(
            "hqk,qhd->khd", grad_scores, queries, preferred_element_type=jnp.float32
        )
        return (grad_query, jnp.stack((grad_key, grad_value)))

    query_zero = jnp.zeros((rows, local_heads, HEAD), jnp.float32)

    def cycle_backward(step, carry):
        pair, grad_query, grad_pair = carry
        source = (own_index - step) % cycle_size
        part_query, part_pair = backward_step(pair, source)
        pair = shifted(pair, "seq", 1)
        grad_pair = shifted((grad_pair + part_pair).astype(jnp.bfloat16), "seq", 1).astype(
            jnp.float32
        )
        return (pair, grad_query + part_query, grad_pair)

    pair_zero = jnp.zeros((2, rows, local_heads, HEAD), jnp.float32)
    pair, grad_query, grad_pair = lax.fori_loop(
        0, cycle_size - 1, cycle_backward, (paired, query_zero, pair_zero)
    )
    last_source = (own_index + 1) % cycle_size
    part_query, part_pair = backward_step(pair, last_source)
    grad_query = grad_query + part_query
    grad_pair = shifted((grad_pair + part_pair).astype(jnp.bfloat16), "seq", 1).astype(jnp.float32)
    width = local_heads * HEAD
    query_low = (grad_query * score_scale).astype(jnp.bfloat16).reshape(rows, width)
    key_low = (grad_pair[0] * score_scale).astype(jnp.bfloat16).reshape(rows, width)
    value_low = grad_pair[1].astype(jnp.bfloat16).reshape(rows, width)
    partial_sum = jnp.dot(query_low, w_query.T, preferred_element_type=jnp.float32)
    partial_sum = partial_sum + jnp.dot(key_low, w_key.T, preferred_element_type=jnp.float32)
    partial_sum = partial_sum + jnp.dot(value_low, w_value.T, preferred_element_type=jnp.float32)
    return lax.psum(partial_sum.astype(jnp.bfloat16), "tp")


def solution(mesh):
    placed = (P("seq", None), P(None, "tp"), P(None, "tp"), P(None, "tp"), P("seq", "tp"))
    return jax.shard_map(
        shards, mesh=mesh, in_specs=placed, out_specs=P("seq", None), check_vma=False
    )
```

profile of v0, /device:TPU:2, one launch (start us, length us, event | category | flops | bytes accessed | tf_op | source)
XLA Modules:
  0.0 712.7 jit_solution(14438093139279428678)
XLA Ops:
  8.5 3.0 convolution_convert_fusion.2
  17.0 2.9 convolution_convert_fusion
  27.3 186.8 %while.45 = (s32[]{:T(128)}, bf16[2,384,2,128]{3,1,2,0:T(8,128)(2,1)}, f32[2,384]{1,0:T(2,128)S(1)}, f32[2,384]{1,0:T(2,128)S(1)}, f32[2,384,128]{2,1,0:T(8,128)...) while((s32[]{:T(128)}, ...), condition=%wide.region_5.6_spmd.clone.clone, body=%wide.region_2.5_spmd.clone.clone.sunk | while | flops 153406096 | bytes 10770766 | solution.py:69
  27.4 7.3 %collective-permute-done = bf16[2,384,2,128]{3,1,2,0:T(8,128)(2,1)S(1)} collective-permute-done((bf16[2,384,2,128]{3,1,2,0:T(8,128)(2,1)}, bf16[2,384,2,128]{3,1,2,0:T(8,128)(2,1)S(1)}, u32[]{:S(2)}, u32[]{:S(2)}) %collective-permute-start) | collective-permute-done | bytes 393248 | tf_op jit(solution)/shard_map/while/body/eval_jaxpr/ppermute | solution.py:12
  38.4 7.3 %collective-permute-done = bf16[2,384,2,128]{3,1,2,0:T(8,128)(2,1)S(1)} collective-permute-done((bf16[2,384,2,128]{3,1,2,0:T(8,128)(2,1)}, bf16[2,384,2,128]{3,1,2,0:T(8,128)(2,1)S(1)}, u32[]{:S(2)}, u32[]{:S(2)}) %collective-permute-start) | collective-permute-done | bytes 393248 | tf_op jit(solution)/shard_map/while/body/eval_jaxpr/ppermute | solution.py:12
  49.6 7.1 collective-permute-done
  61.4 6.2 collective-permute-done
  73.3 6.3 collective-permute-done
  85.2 7.5 %collective-permute-done = bf16[2,384,2,128]{3,1,2,0:T(8,128)(2,1)S(1)} collective-permute-done((bf16[2,384,2,128]{3,1,2,0:T(8,128)(2,1)}, bf16[2,384,2,128]{3,1,2,0:T(8,128)(2,1)S(1)}, u32[]{:S(2)}, u32[]{:S(2)}) %collective-permute-start) | collective-permute-done | bytes 393248 | tf_op jit(solution)/shard_map/while/body/eval_jaxpr/ppermute | solution.py:12
  97.1 8.7 %collective-permute-done = bf16[2,384,2,128]{3,1,2,0:T(8,128)(2,1)S(1)} collective-permute-done((bf16[2,384,2,128]{3,1,2,0:T(8,128)(2,1)}, bf16[2,384,2,128]{3,1,2,0:T(8,128)(2,1)S(1)}, u32[]{:S(2)}, u32[]{:S(2)}) %collective-permute-start) | collective-permute-done | bytes 393248 | tf_op jit(solution)/shard_map/while/body/eval_jaxpr/ppermute | solution.py:12
  109.5 9.4 %collective-permute-done = bf16[2,384,2,128]{3,1,2,0:T(8,128)(2,1)S(1)} collective-permute-done((bf16[2,384,2,128]{3,1,2,0:T(8,128)(2,1)}, bf16[2,384,2,128]{3,1,2,0:T(8,128)(2,1)S(1)}, u32[]{:S(2)}, u32[]{:S(2)}) %collective-permute-start) | collective-permute-done | bytes 393248 | tf_op jit(solution)/shard_map/while/body/eval_jaxpr/ppermute | solution.py:12
  122.6 9.4 %collective-permute-done = bf16[2,384,2,128]{3,1,2,0:T(8,128)(2,1)S(1)} collective-permute-done((bf16[2,384,2,128]{3,1,2,0:T(8,128)(2,1)}, bf16[2,384,2,128]{3,1,2,0:T(8,128)(2,1)S(1)}, u32[]{:S(2)}, u32[]{:S(2)}) %collective-permute-start) | collective-permute-done | bytes 393248 | tf_op jit(solution)/shard_map/while/body/eval_jaxpr/ppermute | solution.py:12
  135.7 9.4 %collective-permute-done = bf16[2,384,2,128]{3,1,2,0:T(8,128)(2,1)S(1)} collective-permute-done((bf16[2,384,2,128]{3,1,2,0:T(8,128)(2,1)}, bf16[2,384,2,128]{3,1,2,0:T(8,128)(2,1)S(1)}, u32[]{:S(2)}, u32[]{:S(2)}) %collective-permute-start) | collective-permute-done | bytes 393248 | tf_op jit(solution)/shard_map/while/body/eval_jaxpr/ppermute | solution.py:12
  148.8 9.4 %collective-permute-done = bf16[2,384,2,128]{3,1,2,0:T(8,128)(2,1)S(1)} collective-permute-done((bf16[2,384,2,128]{3,1,2,0:T(8,128)(2,1)}, bf16[2,384,2,128]{3,1,2,0:T(8,128)(2,1)S(1)}, u32[]{:S(2)}, u32[]{:S(2)}) %collective-permute-start) | collective-permute-done | bytes 393248 | tf_op jit(solution)/shard_map/while/body/eval_jaxpr/ppermute | solution.py:12
  161.8 9.4 %collective-permute-done = bf16[2,384,2,128]{3,1,2,0:T(8,128)(2,1)S(1)} collective-permute-done((bf16[2,384,2,128]{3,1,2,0:T(8,128)(2,1)}, bf16[2,384,2,128]{3,1,2,0:T(8,128)(2,1)S(1)}, u32[]{:S(2)}, u32[]{:S(2)}) %collective-permute-start) | collective-permute-done | bytes 393248 | tf_op jit(solution)/shard_map/while/body/eval_jaxpr/ppermute | solution.py:12
  174.9 9.4 %collective-permute-done = bf16[2,384,2,128]{3,1,2,0:T(8,128)(2,1)S(1)} collective-permute-done((bf16[2,384,2,128]{3,1,2,0:T(8,128)(2,1)}, bf16[2,384,2,128]{3,1,2,0:T(8,128)(2,1)S(1)}, u32[]{:S(2)}, u32[]{:S(2)}) %collective-permute-start) | collective-permute-done | bytes 393248 | tf_op jit(solution)/shard_map/while/body/eval_jaxpr/ppermute | solution.py:12
  188.0 9.4 %collective-permute-done = bf16[2,384,2,128]{3,1,2,0:T(8,128)(2,1)S(1)} collective-permute-done((bf16[2,384,2,128]{3,1,2,0:T(8,128)(2,1)}, bf16[2,384,2,128]{3,1,2,0:T(8,128)(2,1)S(1)}, u32[]{:S(2)}, u32[]{:S(2)}) %collective-permute-start) | collective-permute-done | bytes 393248 | tf_op jit(solution)/shard_map/while/body/eval_jaxpr/ppermute | solution.py:12
  201.1 9.4 %collective-permute-done = bf16[2,384,2,128]{3,1,2,0:T(8,128)(2,1)S(1)} collective-permute-done((bf16[2,384,2,128]{3,1,2,0:T(8,128)(2,1)}, bf16[2,384,2,128]{3,1,2,0:T(8,128)(2,1)S(1)}, u32[]{:S(2)}, u32[]{:S(2)}) %collective-permute-start) | collective-permute-done | bytes 393248 | tf_op jit(solution)/shard_map/while/body/eval_jaxpr/ppermute | solution.py:12
  216.2 282.5 %while.46 = (s32[]{:T(128)}, bf16[2,384,2,128]{3,1,2,0:T(8,128)(2,1)}, f32[384,2,128]{2,0,1:T(8,128)}, f32[2,384,2,128]{3,1,2,0:T(8,128)}, s32[]{:T(128)}, /*ind...) while((s32[]{:T(128)}, ...), condition=%wide.region_8.9_spmd.clone.clone.clone, body=%wide.region_7.8_spmd.clone.clone.clone.sunk | while | flops 380880384 | bytes 22720968 | solution.py:114
  223.5 7.5 %collective-permute-done.2 = bf16[2,384,2,128]{3,1,2,0:T(8,128)(2,1)} collective-permute-done((bf16[2,384,2,128]{3,1,2,0:T(8,128)(2,1)}, bf16[2,384,2,128]{3,1,2,0:T(8,128)(2,1)}, u32[]{:S(2)}, u32[]{:S(2)}) %collective-permute-start.2) | collective-permute-done | bytes 393248 | tf_op jit(solution)/shard_map/while/body/eval_jaxpr/ppermute | solution.py:12
  232.9 2.3 collective-permute-done.1
  240.3 2.2 fusion.129
  242.6 5.7 collective-permute-done.2
  250.2 2.3 collective-permute-done.1
  257.6 2.2 fusion.129
  259.8 7.4 %collective-permute-done.2 = bf16[2,384,2,128]{3,1,2,0:T(8,128)(2,1)} collective-permute-done((bf16[2,384,2,128]{3,1,2,0:T(8,128)(2,1)}, bf16[2,384,2,128]{3,1,2,0:T(8,128)(2,1)}, u32[]{:S(2)}, u32[]{:S(2)}) %collective-permute-start.2) | collective-permute-done | bytes 393248 | tf_op jit(solution)/shard_map/while/body/eval_jaxpr/ppermute | solution.py:12
  269.1 2.3 collective-permute-done.1
  276.5 2.2 fusion.129
  278.7 7.4 %collective-permute-done.2 = bf16[2,384,2,128]{3,1,2,0:T(8,128)(2,1)} collective-permute-done((bf16[2,384,2,128]{3,1,2,0:T(8,128)(2,1)}, bf16[2,384,2,128]{3,1,2,0:T(8,128)(2,1)}, u32[]{:S(2)}, u32[]{:S(2)}) %collective-permute-start.2) | collective-permute-done | bytes 393248 | tf_op jit(solution)/shard_map/while/body/eval_jaxpr/ppermute | solution.py:12
  288.0 2.3 collective-permute-done.1
  295.4 2.2 fusion.129
  297.7 7.4 %collective-permute-done.2 = bf16[2,384,2,128]{3,1,2,0:T(8,128)(2,1)} collective-permute-done((bf16[2,384,2,128]{3,1,2,0:T(8,128)(2,1)}, bf16[2,384,2,128]{3,1,2,0:T(8,128)(2,1)}, u32[]{:S(2)}, u32[]{:S(2)}) %collective-permute-start.2) | collective-permute-done | bytes 393248 | tf_op jit(solution)/shard_map/while/body/eval_jaxpr/ppermute | solution.py:12
  307.0 2.3 collective-permute-done.1
  314.4 2.2 fusion.129
  316.6 7.4 %collective-permute-done.2 = bf16[2,384,2,128]{3,1,2,0:T(8,128)(2,1)} collective-permute-done((bf16[2,384,2,128]{3,1,2,0:T(8,128)(2,1)}, bf16[2,384,2,128]{3,1,2,0:T(8,128)(2,1)}, u32[]{:S(2)}, u32[]{:S(2)}) %collective-permute-start.2) | collective-permute-done | bytes 393248 | tf_op jit(solution)/shard_map/while/body/eval_jaxpr/ppermute | solution.py:12
  325.9 2.3 collective-permute-done.1
  333.3 2.2 fusion.129
  335.6 7.4 %collective-permute-done.2 = bf16[2,384,2,128]{3,1,2,0:T(8,128)(2,1)} collective-permute-done((bf16[2,384,2,128]{3,1,2,0:T(8,128)(2,1)}, bf16[2,384,2,128]{3,1,2,0:T(8,128)(2,1)}, u32[]{:S(2)}, u32[]{:S(2)}) %collective-permute-start.2) | collective-permute-done | bytes 393248 | tf_op jit(solution)/shard_map/while/body/eval_jaxpr/ppermute | solution.py:12
  344.9 2.3 collective-permute-done.1
  352.3 2.2 fusion.129
  354.5 7.4 %collective-permute-done.2 = bf16[2,384,2,128]{3,1,2,0:T(8,128)(2,1)} collective-permute-done((bf16[2,384,2,128]{3,1,2,0:T(8,128)(2,1)}, bf16[2,384,2,128]{3,1,2,0:T(8,128)(2,1)}, u32[]{:S(2)}, u32[]{:S(2)}) %collective-permute-start.2) | collective-permute-done | bytes 393248 | tf_op jit(solution)/shard_map/while/body/eval_jaxpr/ppermute | solution.py:12
  363.8 2.3 collective-permute-done.1
  373.4 7.4 %collective-permute-done.2 = bf16[2,384,2,128]{3,1,2,0:T(8,128)(2,1)} collective-permute-done((bf16[2,384,2,128]{3,1,2,0:T(8,128)(2,1)}, bf16[2,384,2,128]{3,1,2,0:T(8,128)(2,1)}, u32[]{:S(2)}, u32[]{:S(2)}) %collective-permute-start.2) | collective-permute-done | bytes 393248 | tf_op jit(solution)/shard_map/while/body/eval_jaxpr/ppermute | solution.py:12
  382.7 2.3 collective-permute-done.1
  392.4 7.4 %collective-permute-done.2 = bf16[2,384,2,128]{3,1,2,0:T(8,128)(2,1)} collective-permute-done((bf16[2,384,2,128]{3,1,2,0:T(8,128)(2,1)}, bf16[2,384,2,128]{3,1,2,0:T(8,128)(2,1)}, u32[]{:S(2)}, u32[]{:S(2)}) %collective-permute-start.2) | collective-permute-done | bytes 393248 | tf_op jit(solution)/shard_map/while/body/eval_jaxpr/ppermute | solution.py:12
  401.7 2.3 collective-permute-done.1
  409.1 2.2 fusion.129
  411.3 7.4 %collective-permute-done.2 = bf16[2,384,2,128]{3,1,2,0:T(8,128)(2,1)} collective-permute-done((bf16[2,384,2,128]{3,1,2,0:T(8,128)(2,1)}, bf16[2,384,2,128]{3,1,2,0:T(8,128)(2,1)}, u32[]{:S(2)}, u32[]{:S(2)}) %collective-permute-start.2) | collective-permute-done | bytes 393248 | tf_op jit(solution)/shard_map/while/body/eval_jaxpr/ppermute | solution.py:12
  420.6 2.3 collective-permute-done.1
  430.3 7.4 %collective-permute-done.2 = bf16[2,384,2,128]{3,1,2,0:T(8,128)(2,1)} collective-permute-done((bf16[2,384,2,128]{3,1,2,0:T(8,128)(2,1)}, bf16[2,384,2,128]{3,1,2,0:T(8,128)(2,1)}, u32[]{:S(2)}, u32[]{:S(2)}) %collective-permute-start.2) | collective-permute-done | bytes 393248 | tf_op jit(solution)/shard_map/while/body/eval_jaxpr/ppermute | solution.py:12
  439.6 2.3 collective-permute-done.1
  449.2 7.4 %collective-permute-done.2 = bf16[2,384,2,128]{3,1,2,0:T(8,128)(2,1)} collective-permute-done((bf16[2,384,2,128]{3,1,2,0:T(8,128)(2,1)}, bf16[2,384,2,128]{3,1,2,0:T(8,128)(2,1)}, u32[]{:S(2)}, u32[]{:S(2)}) %collective-permute-start.2) | collective-permute-done | bytes 393248 | tf_op jit(solution)/shard_map/while/body/eval_jaxpr/ppermute | solution.py:12
  458.5 2.3 collective-permute-done.1
  468.1 7.4 %collective-permute-done.2 = bf16[2,384,2,128]{3,1,2,0:T(8,128)(2,1)} collective-permute-done((bf16[2,384,2,128]{3,1,2,0:T(8,128)(2,1)}, bf16[2,384,2,128]{3,1,2,0:T(8,128)(2,1)}, u32[]{:S(2)}, u32[]{:S(2)}) %collective-permute-start.2) | collective-permute-done | bytes 393248 | tf_op jit(solution)/shard_map/while/body/eval_jaxpr/ppermute | solution.py:12
  477.5 2.3 collective-permute-done.1
  484.9 2.2 fusion.129
  487.1 7.4 %collective-permute-done.2 = bf16[2,384,2,128]{3,1,2,0:T(8,128)(2,1)} collective-permute-done((bf16[2,384,2,128]{3,1,2,0:T(8,128)(2,1)}, bf16[2,384,2,128]{3,1,2,0:T(8,128)(2,1)}, u32[]{:S(2)}, u32[]{:S(2)}) %collective-permute-start.2) | collective-permute-done | bytes 393248 | tf_op jit(solution)/shard_map/while/body/eval_jaxpr/ppermute | solution.py:12
  496.4 2.3 collective-permute-done.1
  503.4 2.3 copy.48
  510.8 2.8 fusion.59
  513.6 4.2 collective-permute-done.3
  520.7 2.7 add_convert_fusion
  523.5 178.5 %all-reduce.2.cloned.1.call-done = bf16[384,4096]{1,0:T(8,128)(2,1)} async-done(((bf16[384,4096]{1,0:T(8,128)(2,1)}), bf16[384,4096]{1,0:T(8,128)(2,1)}) %all-reduce.2.cloned.1.call-update) | async-done | bytes 3145744 | tf_op jit(solution)/shard_map/psum | solution.py:128
  702.0 3.9 copy.92
  (573 shorter events, 208.1 us)
Async XLA Ops:
  6.5 2.0 copy-start
  6.5 695.4 %all-reduce.2.cloned.1.call-start = ((), (), s32[]{:S(2)}) async-start(), calls=%async_computation | async-start | bytes 6291456 | tf_op jit(solution)/shard_map/psum | solution.py:128
  8.5 7.6 %copy-start.8 = (bf16[384,256]{0,1:T(8,128)(2,1)}, bf16[384,256]{0,1:T(8,128)(2,1)S(1)}, u32[]{:S(2)}) copy-start(bf16[384,256]{0,1:T(8,128)(2,1)S(1)} %copy.35) | copy-start | bytes 589828
  8.5 3.0 copy-start.11
  19.9 5.8 copy-start.14
  27.3 7.4 %collective-permute-start = (bf16[2,384,2,128]{3,1,2,0:T(8,128)(2,1)}, bf16[2,384,2,128]{3,1,2,0:T(8,128)(2,1)S(1)}, u32[]{:S(2)}, u32[]{:S(2)}) collective-permute-start(bf16[2,384,2,128]{3,1,2,0:T(8,128)(2,1)} %get-tuple-element.825), channel_id=1, source_target_pairs={{240,0},{0,16},{16,32},{32,48},{48,64},{64,80},{80,96},{96,112},{1... | collective-permute-start | bytes 1179656 | tf_op jit(solution)/shard_map/while/body/eval_jaxpr/ppermute | solution.py:12
  38.2 7.4 %collective-permute-start = (bf16[2,384,2,128]{3,1,2,0:T(8,128)(2,1)}, bf16[2,384,2,128]{3,1,2,0:T(8,128)(2,1)S(1)}, u32[]{:S(2)}, u32[]{:S(2)}) collective-permute-start(bf16[2,384,2,128]{3,1,2,0:T(8,128)(2,1)} %get-tuple-element.825), channel_id=1, source_target_pairs={{240,0},{0,16},{16,32},{32,48},{48,64},{64,80},{80,96},{96,112},{1... | collective-permute-start | bytes 1179656 | tf_op jit(solution)/shard_map/while/body/eval_jaxpr/ppermute | solution.py:12
  49.2 7.4 %collective-permute-start = (bf16[2,384,2,128]{3,1,2,0:T(8,128)(2,1)}, bf16[2,384,2,128]{3,1,2,0:T(8,128)(2,1)S(1)}, u32[]{:S(2)}, u32[]{:S(2)}) collective-permute-start(bf16[2,384,2,128]{3,1,2,0:T(8,128)(2,1)} %get-tuple-element.825), channel_id=1, source_target_pairs={{240,0},{0,16},{16,32},{32,48},{48,64},{64,80},{80,96},{96,112},{1... | collective-permute-start | bytes 1179656 | tf_op jit(solution)/shard_map/while/body/eval_jaxpr/ppermute | solution.py:12
  60.2 7.4 %collective-permute-start = (bf16[2,384,2,128]{3,1,2,0:T(8,128)(2,1)}, bf16[2,384,2,128]{3,1,2,0:T(8,128)(2,1)S(1)}, u32[]{:S(2)}, u32[]{:S(2)}) collective-permute-start(bf16[2,384,2,128]{3,1,2,0:T(8,128)(2,1)} %get-tuple-element.825), channel_id=1, source_target_pairs={{240,0},{0,16},{16,32},{32,48},{48,64},{64,80},{80,96},{96,112},{1... | collective-permute-start | bytes 1179656 | tf_op jit(solution)/shard_map/while/body/eval_jaxpr/ppermute | solution.py:12
  71.2 8.4 %collective-permute-start = (bf16[2,384,2,128]{3,1,2,0:T(8,128)(2,1)}, bf16[2,384,2,128]{3,1,2,0:T(8,128)(2,1)S(1)}, u32[]{:S(2)}, u32[]{:S(2)}) collective-permute-start(bf16[2,384,2,128]{3,1,2,0:T(8,128)(2,1)} %get-tuple-element.825), channel_id=1, source_target_pairs={{240,0},{0,16},{16,32},{32,48},{48,64},{64,80},{80,96},{96,112},{1... | collective-permute-start | bytes 1179656 | tf_op jit(solution)/shard_map/while/body/eval_jaxpr/ppermute | solution.py:12
  83.1 9.5 %collective-permute-start = (bf16[2,384,2,128]{3,1,2,0:T(8,128)(2,1)}, bf16[2,384,2,128]{3,1,2,0:T(8,128)(2,1)S(1)}, u32[]{:S(2)}, u32[]{:S(2)}) collective-permute-start(bf16[2,384,2,128]{3,1,2,0:T(8,128)(2,1)} %get-tuple-element.825), channel_id=1, source_target_pairs={{240,0},{0,16},{16,32},{32,48},{48,64},{64,80},{80,96},{96,112},{1... | collective-permute-start | bytes 1179656 | tf_op jit(solution)/shard_map/while/body/eval_jaxpr/ppermute | solution.py:12
  96.2 9.5 %collective-permute-start = (bf16[2,384,2,128]{3,1,2,0:T(8,128)(2,1)}, bf16[2,384,2,128]{3,1,2,0:T(8,128)(2,1)S(1)}, u32[]{:S(2)}, u32[]{:S(2)}) collective-permute-start(bf16[2,384,2,128]{3,1,2,0:T(8,128)(2,1)} %get-tuple-element.825), channel_id=1, source_target_pairs={{240,0},{0,16},{16,32},{32,48},{48,64},{64,80},{80,96},{96,112},{1... | collective-permute-start | bytes 1179656 | tf_op jit(solution)/shard_map/while/body/eval_jaxpr/ppermute | solution.py:12
  109.3 9.5 %collective-permute-start = (bf16[2,384,2,128]{3,1,2,0:T(8,128)(2,1)}, bf16[2,384,2,128]{3,1,2,0:T(8,128)(2,1)S(1)}, u32[]{:S(2)}, u32[]{:S(2)}) collective-permute-start(bf16[2,384,2,128]{3,1,2,0:T(8,128)(2,1)} %get-tuple-element.825), channel_id=1, source_target_pairs={{240,0},{0,16},{16,32},{32,48},{48,64},{64,80},{80,96},{96,112},{1... | collective-permute-start | bytes 1179656 | tf_op jit(solution)/shard_map/while/body/eval_jaxpr/ppermute | solution.py:12
  122.4 9.5 %collective-permute-start = (bf16[2,384,2,128]{3,1,2,0:T(8,128)(2,1)}, bf16[2,384,2,128]{3,1,2,0:T(8,128)(2,1)S(1)}, u32[]{:S(2)}, u32[]{:S(2)}) collective-permute-start(bf16[2,384,2,128]{3,1,2,0:T(8,128)(2,1)} %get-tuple-element.825), channel_id=1, source_target_pairs={{240,0},{0,16},{16,32},{32,48},{48,64},{64,80},{80,96},{96,112},{1... | collective-permute-start | bytes 1179656 | tf_op jit(solution)/shard_map/while/body/eval_jaxpr/ppermute | solution.py:12
  135.5 9.5 %collective-permute-start = (bf16[2,384,2,128]{3,1,2,0:T(8,128)(2,1)}, bf16[2,384,2,128]{3,1,2,0:T(8,128)(2,1)S(1)}, u32[]{:S(2)}, u32[]{:S(2)}) collective-permute-start(bf16[2,384,2,128]{3,1,2,0:T(8,128)(2,1)} %get-tuple-element.825), channel_id=1, source_target_pairs={{240,0},{0,16},{16,32},{32,48},{48,64},{64,80},{80,96},{96,112},{1... | collective-permute-start | bytes 1179656 | tf_op jit(solution)/shard_map/while/body/eval_jaxpr/ppermute | solution.py:12
  148.6 9.5 %collective-permute-start = (bf16[2,384,2,128]{3,1,2,0:T(8,128)(2,1)}, bf16[2,384,2,128]{3,1,2,0:T(8,128)(2,1)S(1)}, u32[]{:S(2)}, u32[]{:S(2)}) collective-permute-start(bf16[2,384,2,128]{3,1,2,0:T(8,128)(2,1)} %get-tuple-element.825), channel_id=1, source_target_pairs={{240,0},{0,16},{16,32},{32,48},{48,64},{64,80},{80,96},{96,112},{1... | collective-permute-start | bytes 1179656 | tf_op jit(solution)/shard_map/while/body/eval_jaxpr/ppermute | solution.py:12
  161.7 9.5 %collective-permute-start = (bf16[2,384,2,128]{3,1,2,0:T(8,128)(2,1)}, bf16[2,384,2,128]{3,1,2,0:T(8,128)(2,1)S(1)}, u32[]{:S(2)}, u32[]{:S(2)}) collective-permute-start(bf16[2,384,2,128]{3,1,2,0:T(8,128)(2,1)} %get-tuple-element.825), channel_id=1, source_target_pairs={{240,0},{0,16},{16,32},{32,48},{48,64},{64,80},{80,96},{96,112},{1... | collective-permute-start | bytes 1179656 | tf_op jit(solution)/shard_map/while/body/eval_jaxpr/ppermute | solution.py:12
  174.8 9.5 %collective-permute-start = (bf16[2,384,2,128]{3,1,2,0:T(8,128)(2,1)}, bf16[2,384,2,128]{3,1,2,0:T(8,128)(2,1)S(1)}, u32[]{:S(2)}, u32[]{:S(2)}) collective-permute-start(bf16[2,384,2,128]{3,1,2,0:T(8,128)(2,1)} %get-tuple-element.825), channel_id=1, source_target_pairs={{240,0},{0,16},{16,32},{32,48},{48,64},{64,80},{80,96},{96,112},{1... | collective-permute-start | bytes 1179656 | tf_op jit(solution)/shard_map/while/body/eval_jaxpr/ppermute | solution.py:12
  187.9 9.5 %collective-permute-start = (bf16[2,384,2,128]{3,1,2,0:T(8,128)(2,1)}, bf16[2,384,2,128]{3,1,2,0:T(8,128)(2,1)S(1)}, u32[]{:S(2)}, u32[]{:S(2)}) collective-permute-start(bf16[2,384,2,128]{3,1,2,0:T(8,128)(2,1)} %get-tuple-element.825), channel_id=1, source_target_pairs={{240,0},{0,16},{16,32},{32,48},{48,64},{64,80},{80,96},{96,112},{1... | collective-permute-start | bytes 1179656 | tf_op jit(solution)/shard_map/while/body/eval_jaxpr/ppermute | solution.py:12
  201.0 9.5 %collective-permute-start = (bf16[2,384,2,128]{3,1,2,0:T(8,128)(2,1)}, bf16[2,384,2,128]{3,1,2,0:T(8,128)(2,1)S(1)}, u32[]{:S(2)}, u32[]{:S(2)}) collective-permute-start(bf16[2,384,2,128]{3,1,2,0:T(8,128)(2,1)} %get-tuple-element.825), channel_id=1, source_target_pairs={{240,0},{0,16},{16,32},{32,48},{48,64},{64,80},{80,96},{96,112},{1... | collective-permute-start | bytes 1179656 | tf_op jit(solution)/shard_map/while/body/eval_jaxpr/ppermute | solution.py:12
  217.3 1.5 copy-start.3
  221.4 9.6 %collective-permute-start.2 = (bf16[2,384,2,128]{3,1,2,0:T(8,128)(2,1)}, bf16[2,384,2,128]{3,1,2,0:T(8,128)(2,1)}, u32[]{:S(2)}, u32[]{:S(2)}) collective-permute-start(bf16[2,384,2,128]{3,1,2,0:T(8,128)(2,1)} %fusion.130), channel_id=1, source_target_pairs={{240,0},{0,16},{16,32},{32,48},{48,64},{64,80},{80,96},{96,112},{1... | collective-permute-start | bytes 1179656 | tf_op jit(solution)/shard_map/while/body/eval_jaxpr/ppermute | solution.py:12
  221.4 13.8 %collective-permute-start.1 = (bf16[2,384,2,128]{3,1,2,0:T(8,128)(2,1)S(1)}, bf16[2,384,2,128]{3,1,2,0:T(8,128)(2,1)}, u32[]{:S(2)}, u32[]{:S(2)}) collective-permute-start(bf16[2,384,2,128]{3,1,2,0:T(8,128)(2,1)S(1)} %copy.84), channel_id=1, source_target_pairs={{240,0},{0,16},{16,32},{32,48},{48,64},{64,80},{80,96},{96,112},{1... | collective-permute-start | bytes 1179656 | tf_op jit(solution)/shard_map/while/body/eval_jaxpr/ppermute | solution.py:12
  240.3 7.9 %collective-permute-start.2 = (bf16[2,384,2,128]{3,1,2,0:T(8,128)(2,1)}, bf16[2,384,2,128]{3,1,2,0:T(8,128)(2,1)}, u32[]{:S(2)}, u32[]{:S(2)}) collective-permute-start(bf16[2,384,2,128]{3,1,2,0:T(8,128)(2,1)} %fusion.130), channel_id=1, source_target_pairs={{240,0},{0,16},{16,32},{32,48},{48,64},{64,80},{80,96},{96,112},{1... | collective-permute-start | bytes 1179656 | tf_op jit(solution)/shard_map/while/body/eval_jaxpr/ppermute | solution.py:12
  240.3 12.1 %collective-permute-start.1 = (bf16[2,384,2,128]{3,1,2,0:T(8,128)(2,1)S(1)}, bf16[2,384,2,128]{3,1,2,0:T(8,128)(2,1)}, u32[]{:S(2)}, u32[]{:S(2)}) collective-permute-start(bf16[2,384,2,128]{3,1,2,0:T(8,128)(2,1)S(1)} %copy.84), channel_id=1, source_target_pairs={{240,0},{0,16},{16,32},{32,48},{48,64},{64,80},{80,96},{96,112},{1... | collective-permute-start | bytes 1179656 | tf_op jit(solution)/shard_map/while/body/eval_jaxpr/ppermute | solution.py:12
  253.4 1.5 copy-start.3
  257.5 9.6 %collective-permute-start.2 = (bf16[2,384,2,128]{3,1,2,0:T(8,128)(2,1)}, bf16[2,384,2,128]{3,1,2,0:T(8,128)(2,1)}, u32[]{:S(2)}, u32[]{:S(2)}) collective-permute-start(bf16[2,384,2,128]{3,1,2,0:T(8,128)(2,1)} %fusion.130), channel_id=1, source_target_pairs={{240,0},{0,16},{16,32},{32,48},{48,64},{64,80},{80,96},{96,112},{1... | collective-permute-start | bytes 1179656 | tf_op jit(solution)/shard_map/while/body/eval_jaxpr/ppermute | solution.py:12
  257.5 13.8 %collective-permute-start.1 = (bf16[2,384,2,128]{3,1,2,0:T(8,128)(2,1)S(1)}, bf16[2,384,2,128]{3,1,2,0:T(8,128)(2,1)}, u32[]{:S(2)}, u32[]{:S(2)}) collective-permute-start(bf16[2,384,2,128]{3,1,2,0:T(8,128)(2,1)S(1)} %copy.84), channel_id=1, source_target_pairs={{240,0},{0,16},{16,32},{32,48},{48,64},{64,80},{80,96},{96,112},{1... | collective-permute-start | bytes 1179656 | tf_op jit(solution)/shard_map/while/body/eval_jaxpr/ppermute | solution.py:12
  272.4 1.5 copy-start.3
  276.5 9.6 %collective-permute-start.2 = (bf16[2,384,2,128]{3,1,2,0:T(8,128)(2,1)}, bf16[2,384,2,128]{3,1,2,0:T(8,128)(2,1)}, u32[]{:S(2)}, u32[]{:S(2)}) collective-permute-start(bf16[2,384,2,128]{3,1,2,0:T(8,128)(2,1)} %fusion.130), channel_id=1, source_target_pairs={{240,0},{0,16},{16,32},{32,48},{48,64},{64,80},{80,96},{96,112},{1... | collective-permute-start | bytes 1179656 | tf_op jit(solution)/shard_map/while/body/eval_jaxpr/ppermute | solution.py:12
  276.5 13.8 %collective-permute-start.1 = (bf16[2,384,2,128]{3,1,2,0:T(8,128)(2,1)S(1)}, bf16[2,384,2,128]{3,1,2,0:T(8,128)(2,1)}, u32[]{:S(2)}, u32[]{:S(2)}) collective-permute-start(bf16[2,384,2,128]{3,1,2,0:T(8,128)(2,1)S(1)} %copy.84), channel_id=1, source_target_pairs={{240,0},{0,16},{16,32},{32,48},{48,64},{64,80},{80,96},{96,112},{1... | collective-permute-start | bytes 1179656 | tf_op jit(solution)/shard_map/while/body/eval_jaxpr/ppermute | solution.py:12
  295.4 9.6 %collective-permute-start.2 = (bf16[2,384,2,128]{3,1,2,0:T(8,128)(2,1)}, bf16[2,384,2,128]{3,1,2,0:T(8,128)(2,1)}, u32[]{:S(2)}, u32[]{:S(2)}) collective-permute-start(bf16[2,384,2,128]{3,1,2,0:T(8,128)(2,1)} %fusion.130), channel_id=1, source_target_pairs={{240,0},{0,16},{16,32},{32,48},{48,64},{64,80},{80,96},{96,112},{1... | collective-permute-start | bytes 1179656 | tf_op jit(solution)/shard_map/while/body/eval_jaxpr/ppermute | solution.py:12
  295.4 13.8 %collective-permute-start.1 = (bf16[2,384,2,128]{3,1,2,0:T(8,128)(2,1)S(1)}, bf16[2,384,2,128]{3,1,2,0:T(8,128)(2,1)}, u32[]{:S(2)}, u32[]{:S(2)}) collective-permute-start(bf16[2,384,2,128]{3,1,2,0:T(8,128)(2,1)S(1)} %copy.84), channel_id=1, source_target_pairs={{240,0},{0,16},{16,32},{32,48},{48,64},{64,80},{80,96},{96,112},{1... | collective-permute-start | bytes 1179656 | tf_op jit(solution)/shard_map/while/body/eval_jaxpr/ppermute | solution.py:12
  310.3 1.5 copy-start.3
  314.4 9.6 %collective-permute-start.2 = (bf16[2,384,2,128]{3,1,2,0:T(8,128)(2,1)}, bf16[2,384,2,128]{3,1,2,0:T(8,128)(2,1)}, u32[]{:S(2)}, u32[]{:S(2)}) collective-permute-start(bf16[2,384,2,128]{3,1,2,0:T(8,128)(2,1)} %fusion.130), channel_id=1, source_target_pairs={{240,0},{0,16},{16,32},{32,48},{48,64},{64,80},{80,96},{96,112},{1... | collective-permute-start | bytes 1179656 | tf_op jit(solution)/shard_map/while/body/eval_jaxpr/ppermute | solution.py:12
  314.4 13.8 %collective-permute-start.1 = (bf16[2,384,2,128]{3,1,2,0:T(8,128)(2,1)S(1)}, bf16[2,384,2,128]{3,1,2,0:T(8,128)(2,1)}, u32[]{:S(2)}, u32[]{:S(2)}) collective-permute-start(bf16[2,384,2,128]{3,1,2,0:T(8,128)(2,1)S(1)} %copy.84), channel_id=1, source_target_pairs={{240,0},{0,16},{16,32},{32,48},{48,64},{64,80},{80,96},{96,112},{1... | collective-permute-start | bytes 1179656 | tf_op jit(solution)/shard_map/while/body/eval_jaxpr/ppermute | solution.py:12
  329.2 1.5 copy-start.3
  333.3 9.6 %collective-permute-start.2 = (bf16[2,384,2,128]{3,1,2,0:T(8,128)(2,1)}, bf16[2,384,2,128]{3,1,2,0:T(8,128)(2,1)}, u32[]{:S(2)}, u32[]{:S(2)}) collective-permute-start(bf16[2,384,2,128]{3,1,2,0:T(8,128)(2,1)} %fusion.130), channel_id=1, source_target_pairs={{240,0},{0,16},{16,32},{32,48},{48,64},{64,80},{80,96},{96,112},{1... | collective-permute-start | bytes 1179656 | tf_op jit(solution)/shard_map/while/body/eval_jaxpr/ppermute | solution.py:12
  333.3 13.8 %collective-permute-start.1 = (bf16[2,384,2,128]{3,1,2,0:T(8,128)(2,1)S(1)}, bf16[2,384,2,128]{3,1,2,0:T(8,128)(2,1)}, u32[]{:S(2)}, u32[]{:S(2)}) collective-permute-start(bf16[2,384,2,128]{3,1,2,0:T(8,128)(2,1)S(1)} %copy.84), channel_id=1, source_target_pairs={{240,0},{0,16},{16,32},{32,48},{48,64},{64,80},{80,96},{96,112},{1... | collective-permute-start | bytes 1179656 | tf_op jit(solution)/shard_map/while/body/eval_jaxpr/ppermute | solution.py:12
  352.2 9.6 %collective-permute-start.2 = (bf16[2,384,2,128]{3,1,2,0:T(8,128)(2,1)}, bf16[2,384,2,128]{3,1,2,0:T(8,128)(2,1)}, u32[]{:S(2)}, u32[]{:S(2)}) collective-permute-start(bf16[2,384,2,128]{3,1,2,0:T(8,128)(2,1)} %fusion.130), channel_id=1, source_target_pairs={{240,0},{0,16},{16,32},{32,48},{48,64},{64,80},{80,96},{96,112},{1... | collective-permute-start | bytes 1179656 | tf_op jit(solution)/shard_map/while/body/eval_jaxpr/ppermute | solution.py:12
  352.2 13.8 %collective-permute-start.1 = (bf16[2,384,2,128]{3,1,2,0:T(8,128)(2,1)S(1)}, bf16[2,384,2,128]{3,1,2,0:T(8,128)(2,1)}, u32[]{:S(2)}, u32[]{:S(2)}) collective-permute-start(bf16[2,384,2,128]{3,1,2,0:T(8,128)(2,1)S(1)} %copy.84), channel_id=1, source_target_pairs={{240,0},{0,16},{16,32},{32,48},{48,64},{64,80},{80,96},{96,112},{1... | collective-permute-start | bytes 1179656 | tf_op jit(solution)/shard_map/while/body/eval_jaxpr/ppermute | solution.py:12
  367.1 1.5 copy-start.3
  371.2 9.6 %collective-permute-start.2 = (bf16[2,384,2,128]{3,1,2,0:T(8,128)(2,1)}, bf16[2,384,2,128]{3,1,2,0:T(8,128)(2,1)}, u32[]{:S(2)}, u32[]{:S(2)}) collective-permute-start(bf16[2,384,2,128]{3,1,2,0:T(8,128)(2,1)} %fusion.130), channel_id=1, source_target_pairs={{240,0},{0,16},{16,32},{32,48},{48,64},{64,80},{80,96},{96,112},{1... | collective-permute-start | bytes 1179656 | tf_op jit(solution)/shard_map/while/body/eval_jaxpr/ppermute | solution.py:12
  371.2 13.8 %collective-permute-start.1 = (bf16[2,384,2,128]{3,1,2,0:T(8,128)(2,1)S(1)}, bf16[2,384,2,128]{3,1,2,0:T(8,128)(2,1)}, u32[]{:S(2)}, u32[]{:S(2)}) collective-permute-start(bf16[2,384,2,128]{3,1,2,0:T(8,128)(2,1)S(1)} %copy.84), channel_id=1, source_target_pairs={{240,0},{0,16},{16,32},{32,48},{48,64},{64,80},{80,96},{96,112},{1... | collective-permute-start | bytes 1179656 | tf_op jit(solution)/shard_map/while/body/eval_jaxpr/ppermute | solution.py:12
  386.0 1.5 copy-start.3
  390.1 9.6 %collective-permute-start.2 = (bf16[2,384,2,128]{3,1,2,0:T(8,128)(2,1)}, bf16[2,384,2,128]{3,1,2,0:T(8,128)(2,1)}, u32[]{:S(2)}, u32[]{:S(2)}) collective-permute-start(bf16[2,384,2,128]{3,1,2,0:T(8,128)(2,1)} %fusion.130), channel_id=1, source_target_pairs={{240,0},{0,16},{16,32},{32,48},{48,64},{64,80},{80,96},{96,112},{1... | collective-permute-start | bytes 1179656 | tf_op jit(solution)/shard_map/while/body/eval_jaxpr/ppermute | solution.py:12
  390.1 13.8 %collective-permute-start.1 = (bf16[2,384,2,128]{3,1,2,0:T(8,128)(2,1)S(1)}, bf16[2,384,2,128]{3,1,2,0:T(8,128)(2,1)}, u32[]{:S(2)}, u32[]{:S(2)}) collective-permute-start(bf16[2,384,2,128]{3,1,2,0:T(8,128)(2,1)S(1)} %copy.84), channel_id=1, source_target_pairs={{240,0},{0,16},{16,32},{32,48},{48,64},{64,80},{80,96},{96,112},{1... | collective-permute-start | bytes 1179656 | tf_op jit(solution)/shard_map/while/body/eval_jaxpr/ppermute | solution.py:12
  409.1 9.6 %collective-permute-start.2 = (bf16[2,384,2,128]{3,1,2,0:T(8,128)(2,1)}, bf16[2,384,2,128]{3,1,2,0:T(8,128)(2,1)}, u32[]{:S(2)}, u32[]{:S(2)}) collective-permute-start(bf16[2,384,2,128]{3,1,2,0:T(8,128)(2,1)} %fusion.130), channel_id=1, source_target_pairs={{240,0},{0,16},{16,32},{32,48},{48,64},{64,80},{80,96},{96,112},{1... | collective-permute-start | bytes 1179656 | tf_op jit(solution)/shard_map/while/body/eval_jaxpr/ppermute | solution.py:12
  409.1 13.8 %collective-permute-start.1 = (bf16[2,384,2,128]{3,1,2,0:T(8,128)(2,1)S(1)}, bf16[2,384,2,128]{3,1,2,0:T(8,128)(2,1)}, u32[]{:S(2)}, u32[]{:S(2)}) collective-permute-start(bf16[2,384,2,128]{3,1,2,0:T(8,128)(2,1)S(1)} %copy.84), channel_id=1, source_target_pairs={{240,0},{0,16},{16,32},{32,48},{48,64},{64,80},{80,96},{96,112},{1... | collective-permute-start | bytes 1179656 | tf_op jit(solution)/shard_map/while/body/eval_jaxpr/ppermute | solution.py:12
  423.9 1.5 copy-start.3
  428.0 9.6 %collective-permute-start.2 = (bf16[2,384,2,128]{3,1,2,0:T(8,128)(2,1)}, bf16[2,384,2,128]{3,1,2,0:T(8,128)(2,1)}, u32[]{:S(2)}, u32[]{:S(2)}) collective-permute-start(bf16[2,384,2,128]{3,1,2,0:T(8,128)(2,1)} %fusion.130), channel_id=1, source_target_pairs={{240,0},{0,16},{16,32},{32,48},{48,64},{64,80},{80,96},{96,112},{1... | collective-permute-start | bytes 1179656 | tf_op jit(solution)/shard_map/while/body/eval_jaxpr/ppermute | solution.py:12
  428.0 13.8 %collective-permute-start.1 = (bf16[2,384,2,128]{3,1,2,0:T(8,128)(2,1)S(1)}, bf16[2,384,2,128]{3,1,2,0:T(8,128)(2,1)}, u32[]{:S(2)}, u32[]{:S(2)}) collective-permute-start(bf16[2,384,2,128]{3,1,2,0:T(8,128)(2,1)S(1)} %copy.84), channel_id=1, source_target_pairs={{240,0},{0,16},{16,32},{32,48},{48,64},{64,80},{80,96},{96,112},{1... | collective-permute-start | bytes 1179656 | tf_op jit(solution)/shard_map/while/body/eval_jaxpr/ppermute | solution.py:12
  447.0 9.6 %collective-permute-start.2 = (bf16[2,384,2,128]{3,1,2,0:T(8,128)(2,1)}, bf16[2,384,2,128]{3,1,2,0:T(8,128)(2,1)}, u32[]{:S(2)}, u32[]{:S(2)}) collective-permute-start(bf16[2,384,2,128]{3,1,2,0:T(8,128)(2,1)} %fusion.130), channel_id=1, source_target_pairs={{240,0},{0,16},{16,32},{32,48},{48,64},{64,80},{80,96},{96,112},{1... | collective-permute-start | bytes 1179656 | tf_op jit(solution)/shard_map/while/body/eval_jaxpr/ppermute | solution.py:12
  447.0 13.8 %collective-permute-start.1 = (bf16[2,384,2,128]{3,1,2,0:T(8,128)(2,1)S(1)}, bf16[2,384,2,128]{3,1,2,0:T(8,128)(2,1)}, u32[]{:S(2)}, u32[]{:S(2)}) collective-permute-start(bf16[2,384,2,128]{3,1,2,0:T(8,128)(2,1)S(1)} %copy.84), channel_id=1, source_target_pairs={{240,0},{0,16},{16,32},{32,48},{48,64},{64,80},{80,96},{96,112},{1... | collective-permute-start | bytes 1179656 | tf_op jit(solution)/shard_map/while/body/eval_jaxpr/ppermute | solution.py:12
  465.9 9.6 %collective-permute-start.2 = (bf16[2,384,2,128]{3,1,2,0:T(8,128)(2,1)}, bf16[2,384,2,128]{3,1,2,0:T(8,128)(2,1)}, u32[]{:S(2)}, u32[]{:S(2)}) collective-permute-start(bf16[2,384,2,128]{3,1,2,0:T(8,128)(2,1)} %fusion.130), channel_id=1, source_target_pairs={{240,0},{0,16},{16,32},{32,48},{48,64},{64,80},{80,96},{96,112},{1... | collective-permute-start | bytes 1179656 | tf_op jit(solution)/shard_map/while/body/eval_jaxpr/ppermute | solution.py:12
  465.9 13.8 %collective-permute-start.1 = (bf16[2,384,2,128]{3,1,2,0:T(8,128)(2,1)S(1)}, bf16[2,384,2,128]{3,1,2,0:T(8,128)(2,1)}, u32[]{:S(2)}, u32[]{:S(2)}) collective-permute-start(bf16[2,384,2,128]{3,1,2,0:T(8,128)(2,1)S(1)} %copy.84), channel_id=1, source_target_pairs={{240,0},{0,16},{16,32},{32,48},{48,64},{64,80},{80,96},{96,112},{1... | collective-permute-start | bytes 1179656 | tf_op jit(solution)/shard_map/while/body/eval_jaxpr/ppermute | solution.py:12
  480.7 1.5 copy-start.3
  484.8 9.6 %collective-permute-start.2 = (bf16[2,384,2,128]{3,1,2,0:T(8,128)(2,1)}, bf16[2,384,2,128]{3,1,2,0:T(8,128)(2,1)}, u32[]{:S(2)}, u32[]{:S(2)}) collective-permute-start(bf16[2,384,2,128]{3,1,2,0:T(8,128)(2,1)} %fusion.130), channel_id=1, source_target_pairs={{240,0},{0,16},{16,32},{32,48},{48,64},{64,80},{80,96},{96,112},{1... | collective-permute-start | bytes 1179656 | tf_op jit(solution)/shard_map/while/body/eval_jaxpr/ppermute | solution.py:12
  484.8 13.8 %collective-permute-start.1 = (bf16[2,384,2,128]{3,1,2,0:T(8,128)(2,1)S(1)}, bf16[2,384,2,128]{3,1,2,0:T(8,128)(2,1)}, u32[]{:S(2)}, u32[]{:S(2)}) collective-permute-start(bf16[2,384,2,128]{3,1,2,0:T(8,128)(2,1)S(1)} %copy.84), channel_id=1, source_target_pairs={{240,0},{0,16},{16,32},{32,48},{48,64},{64,80},{80,96},{96,112},{1... | collective-permute-start | bytes 1179656 | tf_op jit(solution)/shard_map/while/body/eval_jaxpr/ppermute | solution.py:12
  498.7 1.6 copy-start.9
  503.4 2.3 copy-start.15
  508.1 9.6 %collective-permute-start.3 = (bf16[2,384,2,128]{1,3,2,0:T(8,128)(2,1)}, bf16[2,384,2,128]{1,3,2,0:T(8,128)(2,1)}, u32[]{:S(2)}, u32[]{:S(2)}) collective-permute-start(bf16[2,384,2,128]{1,3,2,0:T(8,128)(2,1)} %fusion.43), channel_id=1, source_target_pairs={{240,0},{0,16},{16,32},{32,48},{48,64},{64,80},{80,96},{96,112},{1... | collective-permute-start | bytes 1179656 | tf_op jit(solution)/shard_map/ppermute | solution.py:12
  510.8 7.9 %copy-start.13 = (bf16[4096,256]{1,0:T(8,128)(2,1)S(1)}, bf16[4096,256]{1,0:T(8,128)(2,1)}, u32[]{:S(2)}) copy-start(bf16[4096,256]{1,0:T(8,128)(2,1)} %param.11) | copy-start | bytes 6291460
  518.7 2.0 copy-start.12
  (85 other events, 92.4 us)
Sparse Core Ops, SparseCore 0:
  523.6 178.3 all-reduce.1
where the time goes:
time: 719 us; the launch traced here: 713 us
  waiting for transfers between devices  451 us (63%)
  matrix products  121 us (17%)
  local copies, waits for them, and re-layouts  64.2 us (9%)
  other arithmetic  54.7 us (8%)
  between operations  13.6 us (2%)
    ppermute x46, waiting for transfers between devices, shifted(): return lax.ppermute(block, axis, route)  273 us
    psum x1, waiting for transfers between devices, shards(): return lax.psum(partial_sum.astype(jnp.bfloat16), 'tp')  178 us
    while x225, local copies, waits for them, and re-layouts  46.5 us
    dot_general x32, matrix products, block_scores(): jnp.einsum('qhd,khd->hqk', queries, key_block, preferred_element_type=jnp...  42.2 us
    dot_general x16, matrix products, backward_step(): jnp.einsum('hqk,khd->qhd', grad_scores, key_block, preferred_element_type...  35 us
    convert_element_type x15, other arithmetic, cycle_backward(): shifted((grad_pair + part_pair).astype(jnp.bfloat16), 'seq', 1)  28.9 us
  transfers between devices with their start and end apart: 47, of which 47 were waited for; matrix products, arithmetic and copies ran while one was open for 10% of the time, Pallas kernels for 0%

commit v1 on v0

v1 whole, which is shorter than its diff:
```python
import functools

import jax
import jax.numpy as jnp
from jax import lax
from jax.experimental import pallas as pl
from jax.experimental.pallas import tpu as pltpu
from jax.sharding import PartitionSpec as P

MESH = pl.DeviceIdType.MESH
HEAD = 128
ROWS = 384
D = 4096
SUB = 3
F32 = jnp.float32
BF16 = jnp.bfloat16
LOG2E = 1.4426950408889634
SCALE = HEAD ** (-0.5)
NEG = -1e30
FLOOR = -1e29
COPIES = 160
LOCALS = 48
HALF = ROWS // 2


def nt(a, b):
    return lax.dot_general(a, b, (((1,), (1,)), ((), ())), preferred_element_type=F32)


def nn(a, b):
    return jnp.dot(a, b, preferred_element_type=F32)


def kernel(
    tok, wq, wk, wv, do, out,
    tok_v, wq_v, wk_v, wv_v,
    q_own, k_own, v_own,
    q_all, do_all, k_all, v_all, k_t,
    key_time, w_s, dp_s, stat, row_tx, row_rx, row_all,
    p_buf, ds_buf, dk_acc, dv_acc,
    dq_tx, dkv_tx, dq_rx, dkv_rx, grads,
    x_tx, x_rx, b_tx, b_rx, a_tx, a_rx, swap_tx, swap_rx, out_b, out_a,
    send_sem, recv_sem, local_sem,
):
    s = lax.axis_index("seq")
    t = lax.axis_index("tp")
    y, xl, c = s // 4, lax.rem(s // 2, 2), lax.rem(s, 2)
    xh, z = t // 8, lax.rem(t, 8)

    def dev(dy=0, dx=0, dc=0, dh=0, dz=0):
        seq = lax.rem(y + dy, 4) * 4 + lax.rem(xl + dx, 2) * 2 + lax.rem(c + dc, 2)
        return (seq, lax.rem(xh + dh, 2) * 8 + lax.rem(z + dz + 8, 8))

    started = []
    counts = [0, 0]

    def send(src, dst, to):
        i = counts[0]
        counts[0] += 1
        copy = pltpu.make_async_remote_copy(
            src_ref=src, dst_ref=dst, send_sem=send_sem.at[i], recv_sem=recv_sem.at[i],
            device_id=to, device_id_type=MESH,
        )
        copy.start()
        started.append(copy)
        return copy

    def local(src, dst):
        i = counts[1]
        counts[1] += 1
        copy = pltpu.make_async_copy(src, dst, local_sem.at[i])
        copy.start()
        return copy

    load_tok = local(tok, tok_v)
    load_k = local(wk, wk_v)
    load_v = local(wv, wv_v)
    load_q = local(wq, wq_v)

    barrier = pltpu.get_barrier_semaphore()
    partners = [dev(dy=dy, dc=dc) for dy in range(4) for dc in range(2) if dy or dc]
    partners += [dev(dx=1, dc=dc) for dc in range(2)]
    partners += [dev(dz=1), dev(dz=-1), dev(dh=1)]
    for partner in partners:
        pl.semaphore_signal(barrier, inc=1, device_id=partner, device_id_type=MESH)
    pl.semaphore_wait(barrier, len(partners))

    def other(e):
        return lax.rem(c + e, 2)

    def query_rows(dy):
        return pl.ds(pl.multiple_of(((4 - dy) % 4) * 256 + c * 128, 128), 128)

    key_rows = pl.ds(pl.multiple_of((xl * 2 + c) * 128, 128), 128)
    order = [(0, 1), (1, 0), (1, 1), (3, 0), (3, 1), (2, 0), (2, 1)]

    def head_lanes(e):
        return pl.ds(pl.multiple_of(other(e) * 128, 128), 128)

    got_do = {(0, 0): local(do.at[:, :, head_lanes(0)], do_all.at[:, query_rows(0), :])}
    for dy, e in order:
        got_do[dy, e] = send(
            do.at[:, :, head_lanes(e)], do_all.at[:, query_rows(dy), :], dev(dy=dy, dc=e)
        )

    def project(weight, own):
        product = nn(tok_v[...], weight[...]).astype(BF16)
        for h in range(2):
            for a in range(SUB):
                own[h, a] = product[a * 128 : (a + 1) * 128, h * 128 : (h + 1) * 128]

    def share_keys(own, everyone):
        copies = [local(own.at[c], everyone.at[:, key_rows, :])]
        for dx, e in ((1, 0), (1, 1), (0, 1)):
            copies.append(send(own.at[other(e)], everyone.at[:, key_rows, :], dev(dx=dx, dc=e)))
        return copies

    load_tok.wait()
    load_k.wait()
    project(wk_v, k_own)
    got_k = share_keys(k_own, k_all)
    load_v.wait()
    project(wv_v, v_own)
    got_v = share_keys(v_own, v_all)
    load_q.wait()
    project(wq_v, q_own)
    got_q = {(0, 0): local(q_own.at[c], q_all.at[:, query_rows(0), :])}
    for dy, e in order:
        got_q[dy, e] = send(q_own.at[other(e)], q_all.at[:, query_rows(dy), :], dev(dy=dy, dc=e))

    row = lax.broadcasted_iota(jnp.int32, (512, 256), 0)
    key_time[...] = (row & 127) * 16 + y * 4 + (row >> 7)

    def arrived(copies):
        copies[0].wait()
        for copy in copies[1:]:
            copy.wait_recv()

    arrived(got_k)
    for a in range(SUB):
        k_t[a] = k_all[a].T
    arrived(got_v)

    exponent = SCALE * LOG2E
    for dq in (0, 3, 1, 2):
        dy = (4 - dq) % 4
        for e in range(2):
            if dy == 0 and e == 0:
                got_q[dy, e].wait()
                got_do[dy, e].wait()
            else:
                got_q[dy, e].wait_recv()
                got_do[dy, e].wait_recv()
        lanes = slice(dq * 256, (dq + 1) * 256)
        col = lax.broadcasted_iota(jnp.int32, (1, 256), 1)
        query_time = (col & 127) * 16 + lax.rem(y + dq, 4) * 4 + xl * 2 + (col >> 7)

        def tile(a, j, slot, masked, lanes=lanes, query_time=query_time):
            scores = nt(k_all[j], q_all[a, lanes, :])
            if masked:
                scores = jnp.where(key_time[...] <= query_time, scores, NEG)
            top = jnp.maximum(jnp.max(scores, axis=0, keepdims=True), FLOOR)
            weights = jnp.exp2((scores - top) * exponent)
            grad_probs = nt(v_all[j], do_all[a, lanes, :])
            stat[slot, 0:1, lanes] = top
            stat[slot, 1:2, lanes] = jnp.sum(weights, axis=0, keepdims=True)
            stat[slot, 2:3, lanes] = jnp.sum(weights * grad_probs, axis=0, keepdims=True)
            w_s[slot, :, lanes] = weights.astype(BF16)
            dp_s[slot, :, lanes] = grad_probs.astype(BF16)

        @pl.loop(0, 3)
        def _(i, tile=tile):
            tile(i, i, i, True)

        @pl.loop(0, 3)
        def _(i, tile=tile):
            tile((i + 3) // 2, i // 2, i + 3, False)

    def slots_of(a):
        return [(j, a if j == a else 2 + a + j) for j in range(a + 1)]

    for a in range(SUB):
        slots = [slot for _, slot in slots_of(a)]
        top = functools.reduce(jnp.maximum, [stat[i, 0:1, :] for i in slots])
        total = jnp.zeros_like(top)
        moment = jnp.zeros_like(top)
        for i in slots:
            factor = jnp.exp2((stat[i, 0:1, :] - top) * exponent)
            total += stat[i, 1:2, :] * factor
            moment += stat[i, 2:3, :] * factor
        some = jnp.maximum(total, 1e-30)
        row_tx[2 * a : 2 * a + 1, :] = top * exponent + jnp.log(some) * LOG2E
        row_tx[2 * a + 1 : 2 * a + 2, :] = moment / some
    row_tx[6:8, :] = jnp.zeros((2, 1024), F32)
    got_rows = {dy: send(row_tx, row_rx.at[3 - dy], dev(dy=dy)) for dy in (1, 3, 2)}
    for dy in (1, 3, 2):
        got_rows[dy].wait_recv()
    for a in range(SUB):
        for dq in range(4):
            lanes = slice(dq * 256, (dq + 1) * 256)
            sums = [row_tx[2 * a : 2 * a + 1, lanes]]
            deltas = [row_tx[2 * a + 1 : 2 * a + 2, lanes]]
            for dy in (1, 2, 3):
                far = ((dq - dy) % 4) * 256
                sums.append(row_rx[dy - 1, 2 * a : 2 * a + 1, far : far + 256])
                deltas.append(row_rx[dy - 1, 2 * a + 1 : 2 * a + 2, far : far + 256])
            top = functools.reduce(jnp.maximum, sums)
            logsum = top + LOG2E * jnp.log(sum(jnp.exp2(v - top) for v in sums))
            row_all[2 * a : 2 * a + 1, lanes] = logsum
            row_all[2 * a + 1 : 2 * a + 2, lanes] = sum(
                d * jnp.exp2(v - logsum) for v, d in zip(sums, deltas)
            )

    got_dq = []
    got_dkv = []
    turn = 0
    for a in (2, 1, 0):
        logsum = row_all[2 * a : 2 * a + 1, :]
        delta = row_all[2 * a + 1 : 2 * a + 2, :]
        grad_q = None
        for j, slot in reversed(slots_of(a)):
            side = turn % 2
            turn += 1
            factor = jnp.exp2(stat[slot, 0:1, :] * exponent - logsum)
            for dq in range(4):
                lanes = slice(dq * 256, (dq + 1) * 256)
                probs = w_s[slot, :, lanes].astype(F32) * factor[:, lanes]
                p_buf[side, :, lanes] = probs.astype(BF16)
                ds_buf[side, :, lanes] = (
                    probs * (dp_s[slot, :, lanes].astype(F32) - delta[:, lanes])
                ).astype(BF16)
            part_v = nn(p_buf[side], do_all[a])
            part_k = nn(ds_buf[side], q_all[a])
            part_q = nn(k_t[j], ds_buf[side])
            grad_q = part_q if grad_q is None else grad_q + part_q
            if a == 2:
                dv_acc[j] = part_v
                dk_acc[j] = part_k
            else:
                dv_acc[j] += part_v
                dk_acc[j] += part_k
        dkv_tx[a, :, 0] = (dk_acc[a] * SCALE).astype(BF16).reshape(4, 128, 128)
        dkv_tx[a, :, 1] = dv_acc[a].astype(BF16).reshape(4, 128, 128)
        dq_tx[a] = (grad_q * SCALE).T.astype(BF16).reshape(4, 2, 128, 128)
        for dx, e in ((1, 0), (1, 1), (0, 1), (0, 0)):
            src = dkv_tx.at[a, lax.rem(xl + dx, 2) * 2 + other(e)]
            dst = dkv_rx.at[a, dx, e]
            if dx or e:
                got_dkv.append(send(src, dst, dev(dx=dx, dc=e)))
            else:
                local(src, dst).wait()
        for dy, e in order[1:] + order[:1] + [(0, 0)]:
            src = dq_tx.at[a, dy, other(e)]
            dst = dq_rx.at[a, (4 - dy) % 4, e]
            if dy or e:
                got_dq.append(send(src, dst, dev(dy=dy, dc=e)))
            else:
                local(src, dst).wait()
    for copy in got_dq + got_dkv:
        copy.wait_recv()
    for a in range(SUB):
        rows = slice(a * 128, (a + 1) * 128)
        for e in range(2):
            base = pl.multiple_of(other(e) * 128, 128)
            total = sum(dq_rx[a, i, e].astype(F32) for i in range(4))
            grads[0, rows, pl.ds(base, 128)] = total.astype(BF16)
            for i in range(2):
                total = dkv_rx[a, 0, e, i].astype(F32) + dkv_rx[a, 1, e, i].astype(F32)
                grads[1 + i, rows, pl.ds(base, 128)] = total.astype(BF16)

    def far(r):
        return lax.rem(z + r + 8, 8)

    def product(start, width):
        rows = pl.ds(pl.multiple_of(start, 128), width)
        return (
            nt(grads[0], wq_v[rows, :]) + nt(grads[1], wk_v[rows, :]) + nt(grads[2], wv_v[rows, :])
        )

    def part_b(r):
        return product(2048 + far(r) * 256, 256)

    def part_a(r, dh):
        return product(lax.rem(xh + dh, 2) * 1024 + far(r) * 128, 128)

    top_rows, low_rows = slice(0, HALF), slice(HALF, ROWS)
    got_x = {}

    def send_x(r):
        x_tx[r + 3] = part_a(r, 1).astype(BF16)
        got_x[r] = send(x_tx.at[r + 3], x_rx.at[r + 3], dev(dh=1))

    got_b = [[None] * 4, [None] * 4]
    got_a = [[None] * 4, [None] * 4]

    def ring_step(step, own, tx, rx, got):
        if step == 0:
            total = own(4).astype(BF16)
            for w, rows in ((0, top_rows), (1, low_rows)):
                tx[w, 0, rows, :] = total[rows]
                got[w][0] = send(
                    tx.at[w, 0, rows, :], rx.at[w, 0, rows, :], dev(dz=1 - 2 * w)
                )
            return
        for w, rows in ((0, top_rows), (1, low_rows)):
            total = own((4 - step) * (1 - 2 * w))
            got[w][step - 1].wait_recv()
            if step == 1:
                tx[w, step] = total.astype(BF16)
                tx[w, step, rows, :] = (total[rows] + rx[w, 0, rows, :].astype(F32)).astype(BF16)
            else:
                tx[w, step] = (total + rx[w, step - 1].astype(F32)).astype(BF16)
            got[w][step] = send(tx.at[w, step], rx.at[w, step], dev(dz=1 - 2 * w))

    def own_a(r):
        term = part_a(r, 0)
        got_x[r].wait_recv()
        return term + x_rx[r + 3].astype(F32)

    send_x(4)
    ring_step(0, part_b, b_tx, b_rx, got_b)
    send_x(3)
    send_x(-3)
    ring_step(1, part_b, b_tx, b_rx, got_b)
    send_x(2)
    send_x(-2)
    ring_step(0, own_a, a_tx, a_rx, got_a)
    send_x(1)
    send_x(-1)
    send_x(0)
    ring_step(2, part_b, b_tx, b_rx, got_b)
    ring_step(1, own_a, a_tx, a_rx, got_a)
    ring_step(3, part_b, b_tx, b_rx, got_b)
    ring_step(2, own_a, a_tx, a_rx, got_a)
    total = part_b(0)
    for w in range(2):
        got_b[w][3].wait_recv()
        total += b_rx[w, 3].astype(F32)
    swap_tx[...] = total.astype(BF16)
    got_swap = send(swap_tx, swap_rx, dev(dh=1))
    ring_step(3, own_a, a_tx, a_rx, got_a)

    stores = []
    gather_b = [[None] * 4, [None] * 4]
    gather_a = [[None] * 4, [None] * 4]
    got_across = {}

    def store_b(r):
        i = far(r)
        lanes = pl.ds(pl.multiple_of(2048 + i * 256, 128), 256)
        stores.append(local(out_b.at[i], out.at[:, lanes]))

    def store_a(r, dh):
        i, h = far(r), lax.rem(xh + dh, 2)
        lanes = pl.ds(pl.multiple_of(h * 1024 + i * 128, 128), 128)
        stores.append(local(out_a.at[h, i], out.at[:, lanes]))

    def pass_on(step, buf, got):
        for w, rows in ((0, top_rows), (1, low_rows)):
            i = far(-step * (1 - 2 * w))
            piece = buf.at[i, rows, :] if step == 3 else buf.at[i]
            got[w][step] = send(piece, piece, dev(dz=1 - 2 * w))

    def across(r):
        i = far(r)
        got_across[r] = send(out_a.at[xh, i], out_a.at[xh, i], dev(dh=1))

    got_swap.wait_recv()
    out_b[z] = (swap_tx[...].astype(F32) + swap_rx[...].astype(F32)).astype(BF16)
    pass_on(0, out_b, gather_b)
    store_b(0)
    total = own_a(0)
    for w in range(2):
        got_a[w][3].wait_recv()
        total += a_rx[w, 3].astype(F32)
    out_a[xh, z] = total.astype(BF16)
    pass_on(0, out_a.at[xh], gather_a)
    across(0)
    store_a(0, 0)
    for step in range(4):
        places = [-step - 1, step + 1] if step < 3 else [4]
        for w in range(2):
            gather_b[w][step].wait_recv()
        if step < 3:
            pass_on(step + 1, out_b, gather_b)
        for r in places:
            store_b(r)
        for w in range(2):
            gather_a[w][step].wait_recv()
        if step < 3:
            pass_on(step + 1, out_a.at[xh], gather_a)
        for r in places:
            across(r)
            store_a(r, 0)
    for r in (0, -1, 1, -2, 2, -3, 3, 4):
        got_across[r].wait_recv()
        store_a(r, 1)
    for copy in stores:
        copy.wait()
    for copy in started:
        copy.wait_send()


def shards(tokens, w_query, w_key, w_value, grad_out):
    anywhere = pl.BlockSpec(memory_space=pl.ANY)
    scratch = [
        ((ROWS, D), BF16), ((D, 256), BF16), ((D, 256), BF16), ((D, 256), BF16),
        ((2, SUB, 128, 128), BF16), ((2, SUB, 128, 128), BF16), ((2, SUB, 128, 128), BF16),
        ((SUB, 1024, 128), BF16), ((SUB, 1024, 128), BF16),
        ((SUB, 512, 128), BF16), ((SUB, 512, 128), BF16), ((SUB, 128, 512), BF16),
        ((512, 256), jnp.int32), ((6, 512, 1024), BF16), ((6, 512, 1024), BF16),
        ((6, 8, 1024), F32), ((8, 1024), F32), ((3, 8, 1024), F32), ((8, 1024), F32),
        ((2, 512, 1024), BF16), ((2, 512, 1024), BF16), ((SUB, 512, 128), F32), ((SUB, 512, 128), F32),
        ((SUB, 4, 2, 128, 128), BF16), ((SUB, 4, 2, 128, 128), BF16),
        ((SUB, 4, 2, 128, 128), BF16), ((SUB, 2, 2, 2, 128, 128), BF16), ((3, ROWS, 256), BF16),
        ((8, ROWS, 128), BF16), ((8, ROWS, 128), BF16),
        ((2, 4, ROWS, 256), BF16), ((2, 4, ROWS, 256), BF16),
        ((2, 4, ROWS, 128), BF16), ((2, 4, ROWS, 128), BF16),
        ((ROWS, 256), BF16), ((ROWS, 256), BF16),
        ((8, ROWS, 256), BF16), ((2, 8, ROWS, 128), BF16),
    ]
    return pl.pallas_call(
        kernel,
        out_shape=jax.ShapeDtypeStruct((ROWS, D), BF16),
        in_specs=[anywhere] * 5,
        out_specs=anywhere,
        scratch_shapes=[pltpu.VMEM(shape, kind) for shape, kind in scratch]
        + [
            pltpu.SemaphoreType.DMA((COPIES,)),
            pltpu.SemaphoreType.DMA((COPIES,)),
            pltpu.SemaphoreType.DMA((LOCALS,)),
        ],
        compiler_params=pltpu.CompilerParams(
            collective_id=0, has_side_effects=True, vmem_limit_bytes=60 * 2**20
        ),
    )(tokens, w_query, w_key, w_value, grad_out.reshape(SUB, 128, 256))


def solution(mesh):
    placed = (P("seq", None), P(None, "tp"), P(None, "tp"), P(None, "tp"), P("seq", "tp"))
    return jax.shard_map(
        shards, mesh=mesh, in_specs=placed, out_specs=P("seq", None), check_vma=False
    )
```

time: 719 us -> 118 us (0.16)
  waiting for transfers between devices: 451 us -> 0 us
  matrix products: 121 us -> 0 us
  Pallas kernels: 0 us -> 114 us
  local copies, waits for them, and re-layouts: 64.2 us -> 3.91 us
  other arithmetic: 54.7 us -> 0 us
  between operations: 13.6 us -> 0.01 us
    ppermute x46 -> x0, waiting for transfers between devices: 273 us -> none  [shifted(): return lax.ppermute(block, axis, route)]
    psum x1 -> x0, waiting for transfers between devices: 178 us -> none  [shards(): return lax.psum(partial_sum.astype(jnp.bfloat16), 'tp')]
    dot_general x118 -> x0, matrix products: 121 us -> none  [the longest x32 42.2 us: block_scores(): jnp.einsum('qhd,khd->hqk', queries, key_block, preferred_element_type=jnp...]
    pallas_call x0 -> x1, Pallas kernels: none -> 114 us  [shards(): pl.pallas_call(kernel, out_shape=jax.ShapeDtypeStruct((ROWS, D), BF16), i...]
    while x228 -> x0, local copies, waits for them, and re-layouts: 50.9 us -> none
    convert_element_type x32 -> x0, other arithmetic: 43.3 us -> none  [the longest x15 28.9 us: cycle_backward(): shifted((grad_pair + part_pair).astype(jnp.bfloat16), 'seq', 1)]
  transfers between devices with their start and end apart: 47 -> 0, of which waited for: 47 -> 0; matrix products, arithmetic and copies ran while one was open for 10% -> 0% of each run, Pallas kernels for 0% -> 0%
where the time goes in v1:
time: 118 us
  Pallas kernels  114 us (97%)
  local copies, waits for them, and re-layouts  3.91 us (3%)
    pallas_call x1, Pallas kernels, shards(): pl.pallas_call(kernel, out_shape=jax.ShapeDtypeStruct((ROWS, D), BF16), i...  114 us
    unnamed x1, local copies, waits for them, and re-layouts  3.91 us

profile of v1, /device:TPU:2, one launch (start us, length us, event | category | flops | bytes accessed | tf_op | source)
XLA Modules:
  0.0 118.0 jit_solution(4271763400808148379)
XLA Ops:
  0.0 114.1 %shard_map.55 = bf16[384,4096]{1,0:T(8,128)(2,1)} custom-call(bf16[384,4096]{1,0:T(8,128)(2,1)} %tok.1, bf16[4096,256]{1,0:T(8,128)(2,1)} %wq.1, bf16[4096,256]{1,0:T(8,128)(2,1)} %wk.1, bf16[4096,256]{1,0:T(8,128)(2,1)} %wv.1, bf16[3,128,256]{2,1,0:T(8,128)(2,1)} %bitcast.1), custom_call_target="tpu_custom_call" | custom-call | tf_op jit(solution)/shard_map/pallas_call | solution.py:422
  114.1 3.9 %copy.7 = bf16[384,4096]{1,0:T(8,128)(2,1)} copy(bf16[384,4096]{1,0:T(8,128)(2,1)} %shard_map.55) | data formatting | bytes 6291456

commit v2 on v1

v2 whole, which is shorter than its diff:
```python
import functools

import jax
import jax.numpy as jnp
from jax import lax
from jax.experimental import pallas as pl
from jax.experimental.pallas import tpu as pltpu
from jax.sharding import PartitionSpec as P

MESH = pl.DeviceIdType.MESH
HEAD = 128
ROWS = 384
D = 4096
SUB = 3
F32 = jnp.float32
BF16 = jnp.bfloat16
LOG2E = 1.4426950408889634
SCALE = HEAD ** (-0.5)
NEG = -1e30
FLOOR = -1e29
COPIES = 200
LOCALS = 48
HALF = ROWS // 2


def nt(a, b):
    return lax.dot_general(a, b, (((1,), (1,)), ((), ())), preferred_element_type=F32)


def nn(a, b):
    return jnp.dot(a, b, preferred_element_type=F32)


def kernel(
    tok, wq, wk, wv, do, out,
    tok_v, wq_v, wk_v, wv_v,
    q_own, k_own, v_own,
    q_all, do_all, k_all, v_all, k_t,
    key_time, w_s, dp_s, tops, totals, moments, row_tx, row_rx, row_all,
    p_buf, ds_buf, dk_acc, dv_acc,
    dq_tx, dkv_tx, dq_rx, dkv_rx, grads,
    x_tx, x_rx, b_tx, b_rx, a_tx, a_rx, swap_tx, swap_rx, out_b, out_a,
    send_sem, recv_sem, local_sem,
):
    s = lax.axis_index("seq")
    t = lax.axis_index("tp")
    y, xl, c = s // 4, lax.rem(s // 2, 2), lax.rem(s, 2)
    xh, z = t // 8, lax.rem(t, 8)

    def dev(dy=0, dx=0, dc=0, dh=0, dz=0):
        seq = lax.rem(y + dy, 4) * 4 + lax.rem(xl + dx, 2) * 2 + lax.rem(c + dc, 2)
        return (seq, lax.rem(xh + dh, 2) * 8 + lax.rem(z + dz + 8, 8))

    started = []
    counts = [0, 0]

    def send(src, dst, to):
        i = counts[0]
        counts[0] += 1
        copy = pltpu.make_async_remote_copy(
            src_ref=src, dst_ref=dst, send_sem=send_sem.at[i], recv_sem=recv_sem.at[i],
            device_id=to, device_id_type=MESH,
        )
        copy.start()
        started.append(copy)
        return copy

    def local(src, dst):
        i = counts[1]
        counts[1] += 1
        copy = pltpu.make_async_copy(src, dst, local_sem.at[i])
        copy.start()
        return copy

    load_tok = local(tok, tok_v)
    load_k = local(wk, wk_v)
    load_v = local(wv, wv_v)
    load_q = local(wq, wq_v)

    barrier = pltpu.get_barrier_semaphore()
    partners = [dev(dy=dy, dc=dc) for dy in range(4) for dc in range(2) if dy or dc]
    partners += [dev(dx=1, dc=dc) for dc in range(2)]
    partners += [dev(dz=1), dev(dz=-1), dev(dh=1)]
    for partner in partners:
        pl.semaphore_signal(barrier, inc=1, device_id=partner, device_id_type=MESH)
    def other(e):
        return lax.rem(c + e, 2)

    def query_rows(dy):
        return pl.ds(pl.multiple_of(((4 - dy) % 4) * 256 + c * 128, 128), 128)

    def key_rows(dx):
        return pl.ds(pl.multiple_of(dx * 256 + c * 128, 128), 128)

    near = [(1, 0), (1, 1), (3, 0), (3, 1)]
    order = [(0, 1), (2, 0), (2, 1)] + near

    def head_lanes(e):
        return pl.ds(pl.multiple_of(other(e) * 128, 128), 128)

    def project(weight, own):
        product = nn(tok_v[...], weight[...]).astype(BF16)
        for h in range(2):
            for a in range(SUB):
                own[h, a] = product[a * 128 : (a + 1) * 128, h * 128 : (h + 1) * 128]

    def share_keys(own, everyone):
        copies = {(0, 0): local(own.at[c], everyone.at[:, key_rows(0), :])}
        for dx, e in ((0, 1), (1, 0), (1, 1)):
            copies[dx, e] = send(own.at[other(e)], everyone.at[:, key_rows(dx), :], dev(dx=dx, dc=e))
        return copies

    load_tok.wait()
    load_k.wait()
    project(wk_v, k_own)
    load_v.wait()
    project(wv_v, v_own)
    load_q.wait()
    project(wq_v, q_own)
    pl.semaphore_wait(barrier, len(partners))
    got_q = {(0, 0): local(q_own.at[c], q_all.at[:, query_rows(0), :])}
    got_do = {(0, 0): local(do.at[:, :, head_lanes(0)], do_all.at[:, query_rows(0), :])}

    def share_q(dy, e):
        got_q[dy, e] = send(q_own.at[other(e)], q_all.at[:, query_rows(dy), :], dev(dy=dy, dc=e))

    def share_do(dy, e):
        got_do[dy, e] = send(
            do.at[:, :, head_lanes(e)], do_all.at[:, query_rows(dy), :], dev(dy=dy, dc=e)
        )

    got_k = share_keys(k_own, k_all)
    share_q(0, 1)
    for e in range(2):
        share_q(1, e)
        share_do(3, e)
    got_v = share_keys(v_own, v_all)
    share_do(0, 1)
    for e in range(2):
        share_do(1, e)
        share_q(3, e)

    row = lax.broadcasted_iota(jnp.int32, (512, 256), 0)
    key_time[...] = (row & 127) * 16 + y * 4 + lax.rem(xl + (row >> 8), 2) * 2 + ((row >> 7) & 1)
    tops[...] = jnp.full(tops.shape, FLOOR, F32)
    totals[...] = jnp.zeros(totals.shape, F32)
    moments[...] = jnp.zeros(moments.shape, F32)

    def arrived(copies, place):
        for e in range(2):
            if place == 0 and e == 0:
                copies[0, 0].wait()
            else:
                copies[place, e].wait_recv()

    exponent = SCALE * LOG2E

    def tiles(dq, f):
        lanes = slice(dq * 256, (dq + 1) * 256)
        rows = slice(f * 256, (f + 1) * 256)
        col = lax.broadcasted_iota(jnp.int32, (1, 256), 1)
        query_time = (col & 127) * 16 + lax.rem(y + dq, 4) * 4 + xl * 2 + (col >> 7)

        def tile(a, j, slot, masked):
            scores = nt(k_all[j, rows, :], q_all[a, lanes, :])
            if masked:
                scores = jnp.where(key_time[rows, :] <= query_time, scores, NEG)
            top = jnp.maximum(jnp.max(scores, axis=0, keepdims=True), FLOOR)
            weights = jnp.exp2((scores - top) * exponent)
            grad_probs = nt(v_all[j, rows, :], do_all[a, lanes, :])
            place = pl.ds(j * 2 + f, 1)
            tops[a, place, lanes] = top
            totals[a, place, lanes] = jnp.sum(weights, axis=0, keepdims=True)
            moments[a, place, lanes] = jnp.sum(weights * grad_probs, axis=0, keepdims=True)
            w_s[slot, rows, lanes] = weights.astype(BF16)
            dp_s[slot, rows, lanes] = grad_probs.astype(BF16)

        @pl.loop(0, 3)
        def _(i):
            tile(i, i, i, True)
            tile((i + 3) // 2, i // 2, i + 3, False)

    arrived(got_k, 0)
    arrived(got_v, 0)
    arrived(got_q, 0)
    arrived(got_do, 0)
    tiles(0, 0)
    arrived(got_q, 1)
    relay_q = send(q_all.at[:, 768:1024, :], q_all.at[:, 512:768, :], dev(dy=1))
    arrived(got_do, 3)
    relay_do = send(do_all.at[:, 256:512, :], do_all.at[:, 512:768, :], dev(dy=3))
    arrived(got_do, 1)
    tiles(3, 0)
    arrived(got_q, 3)
    tiles(1, 0)
    arrived(got_k, 1)
    arrived(got_v, 1)
    for dq in (0, 3, 1):
        tiles(dq, 1)
    for a in range(SUB):
        k_t[a] = k_all[a].T
    relay_q.wait_recv()
    relay_do.wait_recv()
    tiles(2, 0)
    tiles(2, 1)

    def slots_of(a):
        return [(j, a if j == a else 2 + a + j) for j in range(a + 1)]

    row_tx[...] = jnp.zeros(row_tx.shape, F32)
    for a in range(SUB):
        top = jnp.max(tops[a], axis=0, keepdims=True)
        factor = jnp.exp2((tops[a] - top) * exponent)
        total = jnp.maximum(jnp.sum(totals[a] * factor, axis=0, keepdims=True), 1e-30)
        moment = jnp.sum(moments[a] * factor, axis=0, keepdims=True)
        row_tx[a : a + 1, :] = top * exponent + jnp.log(total) * LOG2E
        row_tx[4 + a : 5 + a, :] = moment / total
    got_rows = {dy: send(row_tx, row_rx.at[3 - dy], dev(dy=dy)) for dy in (2, 1, 3)}
    for dy in (1, 3, 2):
        got_rows[dy].wait_recv()
    for dq in range(4):
        lanes = slice(dq * 256, (dq + 1) * 256)
        sums = [row_tx[0:4, lanes]]
        deltas = [row_tx[4:8, lanes]]
        for dy in (1, 2, 3):
            there = ((dq - dy) % 4) * 256
            sums.append(row_rx[dy - 1, 0:4, there : there + 256])
            deltas.append(row_rx[dy - 1, 4:8, there : there + 256])
        top = functools.reduce(jnp.maximum, sums)
        parts = [jnp.exp2(v - top) for v in sums]
        total = sum(parts)
        row_all[0:4, lanes] = top + LOG2E * jnp.log(total)
        row_all[4:8, lanes] = sum(v * part for v, part in zip(deltas, parts)) / total

    got_dq = []
    got_dkv = []
    kept = []
    turn = 0
    for a in (2, 1, 0):
        delta = row_all[4 + a : 5 + a, :]
        factor = jnp.exp2(tops[a] * exponent - row_all[a : a + 1, :])
        grad_q = None
        for j, slot in reversed(slots_of(a)):
            side = turn % 2
            turn += 1
            for dq, f in [(dq, f) for dq in range(4) for f in range(2)]:
                lanes = slice(dq * 256, (dq + 1) * 256)
                rows = slice(f * 256, (f + 1) * 256)
                place = slice(j * 2 + f, j * 2 + f + 1)
                probs = w_s[slot, rows, lanes].astype(F32) * factor[place, lanes]
                p_buf[side, rows, lanes] = probs.astype(BF16)
                ds_buf[side, rows, lanes] = (
                    probs * (dp_s[slot, rows, lanes].astype(F32) - delta[:, lanes])
                ).astype(BF16)
            part_v = nn(p_buf[side], do_all[a])
            part_k = nn(ds_buf[side], q_all[a])
            part_q = nn(k_t[j], ds_buf[side])
            grad_q = part_q if grad_q is None else grad_q + part_q
            if a == 2:
                dv_acc[j] = part_v
                dk_acc[j] = part_k
            else:
                dv_acc[j] += part_v
                dk_acc[j] += part_k
        dkv_tx[a, :, 0] = (dk_acc[a] * SCALE).astype(BF16).reshape(4, 128, 128)
        dkv_tx[a, :, 1] = dv_acc[a].astype(BF16).reshape(4, 128, 128)
        dq_tx[a] = (grad_q * SCALE).T.astype(BF16).reshape(4, 2, 128, 128)
        for dx, e in ((1, 0), (1, 1), (0, 1), (0, 0)):
            src = dkv_tx.at[a, dx * 2 + other(e)]
            dst = dkv_rx.at[a, dx, e]
            if dx or e:
                got_dkv.append(send(src, dst, dev(dx=dx, dc=e)))
            else:
                kept.append(local(src, dst))
        for dy, e in order + [(0, 0)]:
            src = dq_tx.at[a, dy, other(e)]
            dst = dq_rx.at[a, (4 - dy) % 4, e]
            if dy or e:
                got_dq.append(send(src, dst, dev(dy=dy, dc=e)))
            else:
                kept.append(local(src, dst))
    for copy in got_dq + got_dkv:
        copy.wait_recv()
    for copy in kept:
        copy.wait()
    for a in range(SUB):
        rows = slice(a * 128, (a + 1) * 128)
        for e in range(2):
            base = pl.multiple_of(other(e) * 128, 128)
            total = sum(dq_rx[a, i, e].astype(F32) for i in range(4))
            grads[0, rows, pl.ds(base, 128)] = total.astype(BF16)
            for i in range(2):
                total = dkv_rx[a, 0, e, i].astype(F32) + dkv_rx[a, 1, e, i].astype(F32)
                grads[1 + i, rows, pl.ds(base, 128)] = total.astype(BF16)

    def far(r):
        return lax.rem(z + r + 8, 8)

    def product(rows, start, width):
        places = pl.ds(pl.multiple_of(start, 128), width)
        weights = (wq_v, wk_v, wv_v)
        return sum(nt(grads[i, rows, :], weights[i][places, :]) for i in range(3))

    far_way = {0: 0, 1: 1}
    pieces = [slice(p * HALF, (p + 1) * HALF) for p in far_way]

    def rows_of(p, ref, *index):
        return ref.at[(*index, pieces[p], slice(None))]

    def part_b(r, rows):
        return product(rows, 2048 + far(r) * 256, 256)

    def part_a(r, dh, rows):
        return product(rows, lax.rem(xh + dh, 2) * 1024 + far(r) * 128, 128)

    got_x = {}
    arrived_x = set()

    def send_x(r):
        x_tx[r + 3] = part_a(r, 1, slice(None)).astype(BF16)
        got_x[r] = send(x_tx.at[r + 3], x_rx.at[r + 3], dev(dh=1))

    def own_a(r, rows):
        term = part_a(r, 0, rows)
        if r not in arrived_x:
            arrived_x.add(r)
            got_x[r].wait_recv()
        return term + x_rx[r + 3, rows, :].astype(F32)

    class Ring:
        def __init__(self, own, tx, rx):
            self.own, self.tx, self.rx, self.got = own, tx, rx, {}

        def hop(self, w, step, p):
            value = self.own((4 - step) * (1 - 2 * w) if step else 4, pieces[p])
            if (w, step - 1, p) in self.got:
                self.got[w, step - 1, p].wait_recv()
                value += self.rx[w, step - 1, pieces[p], :].astype(F32)
            self.tx[w, step, pieces[p], :] = value.astype(BF16)
            self.got[w, step, p] = send(
                rows_of(p, self.tx, w, step), rows_of(p, self.rx, w, step), dev(dz=1 - 2 * w)
            )

        def wave(self, k):
            for early in (True, False):
                for p, way in far_way.items():
                    for w in range(2):
                        step = k if way == w else k + 1
                        if (way == w) == early and step < 4:
                            self.hop(w, step, p)

        def last(self, p):
            value = self.own(0, pieces[p])
            for w in range(2):
                self.got[w, 3, p].wait_recv()
                value += self.rx[w, 3, pieces[p], :].astype(F32)
            return value

    ring_b = Ring(part_b, b_tx, b_rx)
    ring_a = Ring(own_a, a_tx, a_rx)
    send_x(4)
    ring_b.wave(0)
    for r in (3, -3, 2, -2, 1, -1, 0):
        send_x(r)
    ring_b.wave(1)
    ring_a.wave(0)
    ring_b.wave(2)
    ring_a.wave(1)
    ring_b.wave(3)
    ring_a.wave(2)
    got_swap = []
    for p in far_way:
        swap_tx[pieces[p], :] = ring_b.last(p).astype(BF16)
        got_swap.append(send(rows_of(p, swap_tx), rows_of(p, swap_rx), dev(dh=1)))
    ring_a.wave(3)

    stores = []
    gather_b, gather_a = {}, {}
    got_across = {}

    def store_b(r):
        i = far(r)
        lanes = pl.ds(pl.multiple_of(2048 + i * 256, 128), 256)
        stores.append(local(out_b.at[i], out.at[:, lanes]))

    def store_a(r, dh):
        i, h = far(r), lax.rem(xh + dh, 2)
        lanes = pl.ds(pl.multiple_of(h * 1024 + i * 128, 128), 128)
        stores.append(local(out_a.at[h, i], out.at[:, lanes]))

    def pass_on(got, buf, w, step, p):
        if step:
            got[w, step - 1, p].wait_recv()
        if step < 3 or (step == 3 and far_way[p] == w):
            piece = rows_of(p, buf, far(-step * (1 - 2 * w)))
            got[w, step, p] = send(piece, piece, dev(dz=1 - 2 * w))

    def across(r):
        i = far(r)
        got_across[r] = send(out_a.at[xh, i], out_a.at[xh, i], dev(dh=1))

    own_out_a = out_a.at[xh]
    for p in far_way:
        out_a[xh, z, pieces[p], :] = ring_a.last(p).astype(BF16)
        for w in range(2):
            pass_on(gather_a, own_out_a, w, 0, p)
    across(0)
    store_a(0, 0)
    for p in far_way:
        got_swap[p].wait_recv()
        out_b[z, pieces[p], :] = (
            swap_tx[pieces[p], :].astype(F32) + swap_rx[pieces[p], :].astype(F32)
        ).astype(BF16)
        for w in range(2):
            pass_on(gather_b, out_b, w, 0, p)
    store_b(0)
    for step in range(1, 4):
        for got, buf in ((gather_a, own_out_a), (gather_b, out_b)):
            for p in far_way:
                for w in range(2):
                    pass_on(got, buf, w, step, p)
            for r in (-step, step):
                if got is gather_a:
                    across(r)
                    store_a(r, 0)
                else:
                    store_b(r)
    for p, w in far_way.items():
        gather_a[w, 3, p].wait_recv()
    across(4)
    store_a(4, 0)
    for p, w in far_way.items():
        gather_b[w, 3, p].wait_recv()
    store_b(4)
    for r in (0, -1, 1, -2, 2, -3, 3, 4):
        got_across[r].wait_recv()
        store_a(r, 1)
    for copy in stores:
        copy.wait()
    for copy in started:
        copy.wait_send()


def shards(tokens, w_query, w_key, w_value, grad_out):
    anywhere = pl.BlockSpec(memory_space=pl.ANY)
    scratch = [
        ((ROWS, D), BF16), ((D, 256), BF16), ((D, 256), BF16), ((D, 256), BF16),
        ((2, SUB, 128, 128), BF16), ((2, SUB, 128, 128), BF16), ((2, SUB, 128, 128), BF16),
        ((SUB, 1024, 128), BF16), ((SUB, 1024, 128), BF16),
        ((SUB, 512, 128), BF16), ((SUB, 512, 128), BF16), ((SUB, 128, 512), BF16),
        ((512, 256), jnp.int32), ((6, 512, 1024), BF16), ((6, 512, 1024), BF16),
        ((SUB, 8, 1024), F32), ((SUB, 8, 1024), F32), ((SUB, 8, 1024), F32), ((8, 1024), F32), ((3, 8, 1024), F32), ((8, 1024), F32),
        ((2, 512, 1024), BF16), ((2, 512, 1024), BF16), ((SUB, 512, 128), F32), ((SUB, 512, 128), F32),
        ((SUB, 4, 2, 128, 128), BF16), ((SUB, 4, 2, 128, 128), BF16),
        ((SUB, 4, 2, 128, 128), BF16), ((SUB, 2, 2, 2, 128, 128), BF16), ((3, ROWS, 256), BF16),
        ((8, ROWS, 128), BF16), ((8, ROWS, 128), BF16),
        ((2, 4, ROWS, 256), BF16), ((2, 4, ROWS, 256), BF16),
        ((2, 4, ROWS, 128), BF16), ((2, 4, ROWS, 128), BF16),
        ((ROWS, 256), BF16), ((ROWS, 256), BF16),
        ((8, ROWS, 256), BF16), ((2, 8, ROWS, 128), BF16),
    ]
    return pl.pallas_call(
        kernel,
        out_shape=jax.ShapeDtypeStruct((ROWS, D), BF16),
        in_specs=[anywhere] * 5,
        out_specs=anywhere,
        scratch_shapes=[pltpu.VMEM(shape, kind) for shape, kind in scratch]
        + [
            pltpu.SemaphoreType.DMA((COPIES,)),
            pltpu.SemaphoreType.DMA((COPIES,)),
            pltpu.SemaphoreType.DMA((LOCALS,)),
        ],
        compiler_params=pltpu.CompilerParams(
            collective_id=0, has_side_effects=True, vmem_limit_bytes=60 * 2**20
        ),
    )(tokens, w_query, w_key, w_value, grad_out.reshape(SUB, 128, 256))


def solution(mesh):
    placed = (P("seq", None), P(None, "tp"), P(None, "tp"), P(None, "tp"), P("seq", "tp"))
    return jax.shard_map(
        shards, mesh=mesh, in_specs=placed, out_specs=P("seq", None), check_vma=False
    )
```

time: 118 us -> 112 us (0.949)
  Pallas kernels: 114 us -> 108 us
    pallas_call x1, Pallas kernels: 114 us -> 108 us  [shards(): pl.pallas_call(kernel, out_shape=jax.ShapeDtypeStruct((ROWS, D), BF16), i...]
where the time goes in v2:
time: 112 us
  Pallas kernels  108 us (96%)
  local copies, waits for them, and re-layouts  3.91 us (3%)
    pallas_call x1, Pallas kernels, shards(): pl.pallas_call(kernel, out_shape=jax.ShapeDtypeStruct((ROWS, D), BF16), i...  108 us
    unnamed x1, local copies, waits for them, and re-layouts  3.91 us

profile of v2, /device:TPU:2, one launch (start us, length us, event | category | flops | bytes accessed | tf_op | source)
XLA Modules:
  0.0 112.3 jit_solution(5745471831704940261)
XLA Ops:
  0.0 108.4 %shard_map.55 = bf16[384,4096]{1,0:T(8,128)(2,1)} custom-call(bf16[384,4096]{1,0:T(8,128)(2,1)} %tok.1, bf16[4096,256]{1,0:T(8,128)(2,1)} %wq.1, bf16[4096,256]{1,0:T(8,128)(2,1)} %wk.1, bf16[4096,256]{1,0:T(8,128)(2,1)} %wv.1, bf16[3,128,256]{2,1,0:T(8,128)(2,1)} %bitcast.1), custom_call_target="tpu_custom_call" | custom-call | tf_op jit(solution)/shard_map/pallas_call | solution.py:462
  108.4 3.9 %copy.7 = bf16[384,4096]{1,0:T(8,128)(2,1)} copy(bf16[384,4096]{1,0:T(8,128)(2,1)} %shard_map.55) | data formatting | bytes 6291456

commit v3 on v2

--- a/solution.py
+++ b/solution.py
@@ -18,9 +18,8 @@
 SCALE = HEAD ** (-0.5)
 NEG = -1e30
 FLOOR = -1e29
-COPIES = 200
+COPIES = 240
 LOCALS = 48
-HALF = ROWS // 2
 
 
 def nt(a, b):
@@ -39,7 +38,7 @@
     key_time, w_s, dp_s, tops, totals, moments, row_tx, row_rx, row_all,
     p_buf, ds_buf, dk_acc, dv_acc,
     dq_tx, dkv_tx, dq_rx, dkv_rx, grads,
-    x_tx, x_rx, b_tx, b_rx, a_tx, a_rx, swap_tx, swap_rx, out_b, out_a,
+    x_tx, x_rx, a_own, b_tx, b_rx, a_tx, a_rx, swap_tx, swap_rx, out_b, out_a,
     send_sem, recv_sem, local_sem,
 ):
     s = lax.axis_index("seq")
@@ -232,9 +231,8 @@
         row_all[0:4, lanes] = top + LOG2E * jnp.log(total)
         row_all[4:8, lanes] = sum(v * part for v, part in zip(deltas, parts)) / total
 
-    got_dq = []
-    got_dkv = []
-    kept = []
+    got_grads = {a: [] for a in range(SUB)}
+    kept = {a: [] for a in range(SUB)}
     turn = 0
     for a in (2, 1, 0):
         delta = row_all[4 + a : 5 + a, :]
@@ -269,21 +267,21 @@
             src = dkv_tx.at[a, dx * 2 + other(e)]
             dst = dkv_rx.at[a, dx, e]
             if dx or e:
-                got_dkv.append(send(src, dst, dev(dx=dx, dc=e)))
+                got_grads[a].append(send(src, dst, dev(dx=dx, dc=e)))
             else:
-                kept.append(local(src, dst))
+                kept[a].append(local(src, dst))
         for dy, e in order + [(0, 0)]:
             src = dq_tx.at[a, dy, other(e)]
             dst = dq_rx.at[a, (4 - dy) % 4, e]
             if dy or e:
-                got_dq.append(send(src, dst, dev(dy=dy, dc=e)))
+                got_grads[a].append(send(src, dst, dev(dy=dy, dc=e)))
             else:
-                kept.append(local(src, dst))
-    for copy in got_dq + got_dkv:
-        copy.wait_recv()
-    for copy in kept:
-        copy.wait()
-    for a in range(SUB):
+                kept[a].append(local(src, dst))
+    def finish_grads(a):
+        for copy in got_grads[a]:
+            copy.wait_recv()
+        for copy in kept[a]:
+            copy.wait()
         rows = slice(a * 128, (a + 1) * 128)
         for e in range(2):
             base = pl.multiple_of(other(e) * 128, 128)
@@ -293,46 +291,53 @@
                 total = dkv_rx[a, 0, e, i].astype(F32) + dkv_rx[a, 1, e, i].astype(F32)
                 grads[1 + i, rows, pl.ds(base, 128)] = total.astype(BF16)
 
+    blocks = (2, 1, 0)
+    pieces = [slice(a * 128, (a + 1) * 128) for a in blocks]
+
     def far(r):
         return lax.rem(z + r + 8, 8)
 
-    def product(rows, start, width):
+    def product(p, start, width):
         places = pl.ds(pl.multiple_of(start, 128), width)
         weights = (wq_v, wk_v, wv_v)
-        return sum(nt(grads[i, rows, :], weights[i][places, :]) for i in range(3))
-
-    far_way = {0: 0, 1: 1}
-    pieces = [slice(p * HALF, (p + 1) * HALF) for p in far_way]
+        return sum(nt(grads[i, pieces[p], :], weights[i][places, :]) for i in range(3))
 
     def rows_of(p, ref, *index):
         return ref.at[(*index, pieces[p], slice(None))]
 
-    def part_b(r, rows):
-        return product(rows, 2048 + far(r) * 256, 256)
-
-    def part_a(r, dh, rows):
-        return product(rows, lax.rem(xh + dh, 2) * 1024 + far(r) * 128, 128)
-
     got_x = {}
-    arrived_x = set()
-
-    def send_x(r):
-        x_tx[r + 3] = part_a(r, 1, slice(None)).astype(BF16)
-        got_x[r] = send(x_tx.at[r + 3], x_rx.at[r + 3], dev(dh=1))
-
-    def own_a(r, rows):
-        term = part_a(r, 0, rows)
-        if r not in arrived_x:
-            arrived_x.add(r)
-            got_x[r].wait_recv()
-        return term + x_rx[r + 3, rows, :].astype(F32)
+
+    def start_x(p):
+        theirs = product(p, lax.rem(xh + 1, 2) * 1024, 1024).astype(BF16)
+        for i in range(8):
+            x_tx[i, pieces[p], :] = theirs[:, i * 128 : (i + 1) * 128]
+        mine = product(p, xh * 1024, 1024)
+        for i in range(8):
+            a_own[i, pieces[p], :] = mine[:, i * 128 : (i + 1) * 128]
+
+    def more_x(p, places):
+        for r in places:
+            i = far(r)
+            got_x[r, p] = send(rows_of(p, x_tx, i), rows_of(p, x_rx, i), dev(dh=1))
+
+    def own_b(r, p):
+        return product(p, 2048 + far(r) * 256, 256)
+
+    used_x = set()
+
+    def own_a(r, p):
+        if (r, p) not in used_x:
+            used_x.add((r, p))
+            got_x[r, p].wait_recv()
+        i = far(r)
+        return a_own[i, pieces[p], :] + x_rx[i, pieces[p], :].astype(F32)
 
     class Ring:
-        def __init__(self, own, tx, rx):
-            self.own, self.tx, self.rx, self.got = own, tx, rx, {}
+        def __init__(self, own, tx, rx, far_way):
+            self.own, self.tx, self.rx, self.far_way, self.got = own, tx, rx, far_way, {}
 
         def hop(self, w, step, p):
-            value = self.own((4 - step) * (1 - 2 * w) if step else 4, pieces[p])
+            value = self.own((4 - step) * (1 - 2 * w) if step else 4, p)
             if (w, step - 1, p) in self.got:
                 self.got[w, step - 1, p].wait_recv()
                 value += self.rx[w, step - 1, pieces[p], :].astype(F32)
@@ -341,42 +346,26 @@
                 rows_of(p, self.tx, w, step), rows_of(p, self.rx, w, step), dev(dz=1 - 2 * w)
             )
 
-        def wave(self, k):
-            for early in (True, False):
-                for p, way in far_way.items():
-                    for w in range(2):
-                        step = k if way == w else k + 1
-                        if (way == w) == early and step < 4:
-                            self.hop(w, step, p)
+        def wave(self, k, p):
+            way = self.far_way[p]
+            self.hop(way, k, p)
+            if k < 3:
+                self.hop(1 - way, k + 1, p)
 
         def last(self, p):
-            value = self.own(0, pieces[p])
+            value = self.own(0, p)
             for w in range(2):
                 self.got[w, 3, p].wait_recv()
                 value += self.rx[w, 3, pieces[p], :].astype(F32)
             return value
 
-    ring_b = Ring(part_b, b_tx, b_rx)
-    ring_a = Ring(own_a, a_tx, a_rx)
-    send_x(4)
-    ring_b.wave(0)
-    for r in (3, -3, 2, -2, 1, -1, 0):
-        send_x(r)
-    ring_b.wave(1)
-    ring_a.wave(0)
-    ring_b.wave(2)
-    ring_a.wave(1)
-    ring_b.wave(3)
-    ring_a.wave(2)
-    got_swap = []
-    for p in far_way:
-        swap_tx[pieces[p], :] = ring_b.last(p).astype(BF16)
-        got_swap.append(send(rows_of(p, swap_tx), rows_of(p, swap_rx), dev(dh=1)))
-    ring_a.wave(3)
-
+    ring_b = Ring(own_b, b_tx, b_rx, (0, 1, 0))
+    ring_a = Ring(own_a, a_tx, a_rx, (0, 1, 1))
     stores = []
+    got_swap = {}
     gather_b, gather_a = {}, {}
     got_across = {}
+    own_out_a = out_a.at[xh]
 
     def store_b(r):
         i = far(r)
@@ -388,52 +377,64 @@
         lanes = pl.ds(pl.multiple_of(h * 1024 + i * 128, 128), 128)
         stores.append(local(out_a.at[h, i], out.at[:, lanes]))
 
-    def pass_on(got, buf, w, step, p):
-        if step:
-            got[w, step - 1, p].wait_recv()
-        if step < 3 or (step == 3 and far_way[p] == w):
-            piece = rows_of(p, buf, far(-step * (1 - 2 * w)))
-            got[w, step, p] = send(piece, piece, dev(dz=1 - 2 * w))
-
-    def across(r):
-        i = far(r)
-        got_across[r] = send(out_a.at[xh, i], out_a.at[xh, i], dev(dh=1))
-
-    own_out_a = out_a.at[xh]
-    for p in far_way:
-        out_a[xh, z, pieces[p], :] = ring_a.last(p).astype(BF16)
+    def pass_on(got, buf, far_way, step, p):
         for w in range(2):
-            pass_on(gather_a, own_out_a, w, 0, p)
-    across(0)
-    store_a(0, 0)
-    for p in far_way:
-        got_swap[p].wait_recv()
-        out_b[z, pieces[p], :] = (
-            swap_tx[pieces[p], :].astype(F32) + swap_rx[pieces[p], :].astype(F32)
-        ).astype(BF16)
-        for w in range(2):
-            pass_on(gather_b, out_b, w, 0, p)
-    store_b(0)
-    for step in range(1, 4):
-        for got, buf in ((gather_a, own_out_a), (gather_b, out_b)):
-            for p in far_way:
-                for w in range(2):
-                    pass_on(got, buf, w, step, p)
-            for r in (-step, step):
-                if got is gather_a:
-                    across(r)
+            if step and (step < 4 or far_way[p] == w):
+                got[w, step - 1, p].wait_recv()
+            if step < 3 or (step == 3 and far_way[p] == w):
+                piece = rows_of(p, buf, far(-step * (1 - 2 * w)))
+                got[w, step, p] = send(piece, piece, dev(dz=1 - 2 * w))
+
+    def places(step):
+        return [0] if step == 0 else [4] if step == 4 else [-step, step]
+
+    def stage_b(k, p):
+        if k < 4:
+            ring_b.wave(k, p)
+        elif k == 4:
+            swap_tx[pieces[p], :] = ring_b.last(p).astype(BF16)
+            got_swap[p] = send(rows_of(p, swap_tx), rows_of(p, swap_rx), dev(dh=1))
+        elif k < 10:
+            if k == 5:
+                got_swap[p].wait_recv()
+                out_b[z, pieces[p], :] = (
+                    swap_tx[pieces[p], :].astype(F32) + swap_rx[pieces[p], :].astype(F32)
+                ).astype(BF16)
+            pass_on(gather_b, out_b, ring_b.far_way, k - 5, p)
+            if p == 2:
+                for r in places(k - 5):
+                    store_b(r)
+
+    def stage_a(k, p):
+        if k < 4:
+            ring_a.wave(k, p)
+        elif k < 9:
+            if k == 4:
+                out_a[xh, z, pieces[p], :] = ring_a.last(p).astype(BF16)
+            pass_on(gather_a, own_out_a, ring_a.far_way, k - 4, p)
+            for r in places(k - 4):
+                piece = rows_of(p, out_a, xh, far(r))
+                got_across[r, p] = send(piece, piece, dev(dh=1))
+                if p == 2:
                     store_a(r, 0)
-                else:
-                    store_b(r)
-    for p, w in far_way.items():
-        gather_a[w, 3, p].wait_recv()
-    across(4)
-    store_a(4, 0)
-    for p, w in far_way.items():
-        gather_b[w, 3, p].wait_recv()
-    store_b(4)
+
+    offset = (0, 1, 1)
+    for turn in range(12):
+        for p in (0, 1, 2):
+            if turn == offset[p]:
+                finish_grads(blocks[p])
+            if turn >= offset[p]:
+                stage_b(turn - offset[p], p)
+            if turn == offset[p]:
+                start_x(p)
+            if 0 <= turn - offset[p] < 4:
+                more_x(p, ((4, 3, -3), (2, -2), (1, -1), (0,))[turn - offset[p]])
+        for p in (0, 1, 2):
+            if turn >= offset[p] + 1:
+                stage_a(turn - offset[p] - 1, p)
     for r in (0, -1, 1, -2, 2, -3, 3, 4):
-        got_across[r].wait_recv()
+        for p in range(3):
+            got_across[r, p].wait_recv()
         store_a(r, 1)
     for copy in stores:
         copy.wait()
@@ -453,7 +454,7 @@
         ((2, 512, 1024), BF16), ((2, 512, 1024), BF16), ((SUB, 512, 128), F32), ((SUB, 512, 128), F32),
         ((SUB, 4, 2, 128, 128), BF16), ((SUB, 4, 2, 128, 128), BF16),
         ((SUB, 4, 2, 128, 128), BF16), ((SUB, 2, 2, 2, 128, 128), BF16), ((3, ROWS, 256), BF16),
-        ((8, ROWS, 128), BF16), ((8, ROWS, 128), BF16),
+        ((8, ROWS, 128), BF16), ((8, ROWS, 128), BF16), ((8, ROWS, 128), F32),
         ((2, 4, ROWS, 256), BF16), ((2, 4, ROWS, 256), BF16),
         ((2, 4, ROWS, 128), BF16), ((2, 4, ROWS, 128), BF16),
         ((ROWS, 256), BF16), ((ROWS, 256), BF16),
@@ -461,9 +462,9 @@
     ]
     return pl.pallas_call(
         kernel,
-        out_shape=jax.ShapeDtypeStruct((ROWS, D), BF16),
+        out_shape=pltpu.VMEM((ROWS, D), BF16),
         in_specs=[anywhere] * 5,
-        out_specs=anywhere,
+        out_specs=pl.BlockSpec(memory_space=pltpu.VMEM),
         scratch_shapes=[pltpu.VMEM(shape, kind) for shape, kind in scratch]
         + [
             pltpu.SemaphoreType.DMA((COPIES,)),
@@ -471,7 +472,7 @@
             pltpu.SemaphoreType.DMA((LOCALS,)),
         ],
         compiler_params=pltpu.CompilerParams(
-            collective_id=0, has_side_effects=True, vmem_limit_bytes=60 * 2**20
+            collective_id=0, has_side_effects=True, vmem_limit_bytes=54 * 2**20
         ),
     )(tokens, w_query, w_key, w_value, grad_out.reshape(SUB, 128, 256))
 

time: 112 us -> 107 us (0.955)
  Pallas kernels: 108 us -> 105 us
  local copies, waits for them, and re-layouts: 3.91 us -> 1.67 us
    pallas_call x1, Pallas kernels: 108 us -> 105 us  [shards(): pl.pallas_call(kernel, out_shape=pltpu.VMEM((ROWS, D), BF16), in_specs=[a...]
    unnamed x1, local copies, waits for them, and re-layouts: 3.91 us -> 1.67 us
where the time goes in v3:
time: 107 us
  Pallas kernels  105 us (98%)
  local copies, waits for them, and re-layouts  1.67 us (2%)
    pallas_call x1, Pallas kernels, shards(): pl.pallas_call(kernel, out_shape=pltpu.VMEM((ROWS, D), BF16), in_specs=[a...  105 us

profile of v3, /device:TPU:2, one launch (start us, length us, event | category | flops | bytes accessed | tf_op | source)
XLA Modules:
  0.0 106.8 jit_solution(12567422632595769862)
XLA Ops:
  0.0 105.1 %shard_map.55 = bf16[384,4096]{1,0:T(8,128)(2,1)S(1)} custom-call(bf16[384,4096]{1,0:T(8,128)(2,1)} %tok.1, bf16[4096,256]{1,0:T(8,128)(2,1)} %wq.1, bf16[4096,256]{1,0:T(8,128)(2,1)} %wk.1, bf16[4096,256]{1,0:T(8,128)(2,1)} %wv.1, bf16[3,128,256]{2,1,0:T(8,128)(2,1)} %bitcast.1), custom_call_target="tpu_custom_call" | custom-call | tf_op jit(solution)/shard_map/pallas_call | solution.py:463
  105.1 1.7 %copy.7 = bf16[384,4096]{1,0:T(8,128)(2,1)} copy(bf16[384,4096]{1,0:T(8,128)(2,1)S(1)} %shard_map.55) | data formatting | bytes 6291456

commit v4 on v3

--- a/solution.py
+++ b/solution.py
@@ -420,6 +420,10 @@
 
     offset = (0, 1, 1)
     for turn in range(12):
+        if turn >= 6:
+            for p in (0, 1, 2):
+                if turn >= offset[p] + 1:
+                    stage_a(turn - offset[p] - 1, p)
         for p in (0, 1, 2):
             if turn == offset[p]:
                 finish_grads(blocks[p])
@@ -429,9 +433,10 @@
                 start_x(p)
             if 0 <= turn - offset[p] < 4:
                 more_x(p, ((4, 3, -3), (2, -2), (1, -1), (0,))[turn - offset[p]])
-        for p in (0, 1, 2):
-            if turn >= offset[p] + 1:
-                stage_a(turn - offset[p] - 1, p)
+        if turn < 6:
+            for p in (0, 1, 2):
+                if turn >= offset[p] + 1:
+                    stage_a(turn - offset[p] - 1, p)
     for r in (0, -1, 1, -2, 2, -3, 3, 4):
         for p in range(3):
             got_across[r, p].wait_recv()

time: 107 us -> 106 us (level)
    pallas_call x1, Pallas kernels: 105 us -> 104 us  [shards(): pl.pallas_call(kernel, out_shape=pltpu.VMEM((ROWS, D), BF16), in_specs=[a...]
where the time goes in v4:
time: 106 us; the launch traced here: 105 us
  Pallas kernels  104 us (98%)
  local copies, waits for them, and re-layouts  1.67 us (2%)
    pallas_call x1, Pallas kernels, shards(): pl.pallas_call(kernel, out_shape=pltpu.VMEM((ROWS, D), BF16), in_specs=[a...  104 us

profile of v4, /device:TPU:2, one launch (start us, length us, event | category | flops | bytes accessed | tf_op | source)
XLA Modules:
  0.0 105.5 jit_solution(11272970366751762470)
XLA Ops:
  0.0 103.8 %shard_map.55 = bf16[384,4096]{1,0:T(8,128)(2,1)S(1)} custom-call(bf16[384,4096]{1,0:T(8,128)(2,1)} %tok.1, bf16[4096,256]{1,0:T(8,128)(2,1)} %wq.1, bf16[4096,256]{1,0:T(8,128)(2,1)} %wk.1, bf16[4096,256]{1,0:T(8,128)(2,1)} %wv.1, bf16[3,128,256]{2,1,0:T(8,128)(2,1)} %bitcast.1), custom_call_target="tpu_custom_call" | custom-call | tf_op jit(solution)/shard_map/pallas_call | solution.py:468
  103.8 1.7 %copy.7 = bf16[384,4096]{1,0:T(8,128)(2,1)} copy(bf16[384,4096]{1,0:T(8,128)(2,1)S(1)} %shard_map.55) | data formatting | bytes 6291456
